TPU v7x, 768 devices: a whole 4x8x12 slice. The times are simulated.
768 devices in a mesh: space: 64 (over x, y, core), feat: 12 (over z).
Axes of the slice: x: 4, y: 8, z: 12, core: 2. Of those that a mesh axis runs over, the one named last changes fastest.
Arguments:
- grid_latents: bfloat16 [196608, 512], P(('space', 'feat')), may hold values from -6 to 6
- grid_region: int32 [196608, 1], P(('space', 'feat')), may hold values from 0 to 63; in each aligned block of 256 rows (0 to 255, 256 to 511, ...) at most 8 rows name the same one
- grid_node: int32 [196608], P(('space', 'feat')), may hold values from 0 to 191
- mesh_latents: bfloat16 [12288, 512], P('space'), may hold values from -6 to 6
- edge_latents: bfloat16 [294912, 512], P(('space', 'feat')), may hold values from -6 to 6
- edge_sender: int32 [294912], P(('space', 'feat')), may hold values from 0 to 959, as said below
- edge_receiver: int32 [294912], P(('space', 'feat')), may hold values from 0 to 191
- halo_send: int32 [64, 64, 12], P('space'), may hold values from 0 to 191
- w_grid: bfloat16 [512, 512], replicated, may hold values from -0.25 to 0.25
- w_edge_in: bfloat16 [1536, 512], replicated, may hold values from -0.15625 to 0.15625
- w_edge_out: bfloat16 [512, 512], replicated, may hold values from -0.25 to 0.25
- w_node_in: bfloat16 [1536, 512], replicated, may hold values from -0.15625 to 0.15625
- w_node_out: bfloat16 [512, 512], replicated, may hold values from -0.25 to 0.25
- cot_mesh: bfloat16 [12288, 512], P('space'), may hold values from -6 to 6
- cot_edges: bfloat16 [294912, 512], P(('space', 'feat')), may hold values from -6 to 6
Outputs:
- new_mesh: bfloat16 [12288, 512], P('space')
- new_edges: bfloat16 [294912, 512], P(('space', 'feat'))
- grad_mesh: bfloat16 [12288, 512], P(('space', 'feat'))
- grad_edges: bfloat16 [294912, 512], P(('space', 'feat'))
Inputs may be any that keep to these rules, and one draw needn't show every extreme that they name: `grid_region`: in the 256 grid rows of one device no region is named by more than 8 rows, a bound that some block reaches. `edge_sender`: rows 0 to 191 of the lookup table are the edge's own region's nodes; row 192 + p * 12 + k is halo row k sent by region p.
All inputs are finite; a program needn't handle non-finite values.
Results may differ from a plain program's by a relative error of at most 0.027.
Values may be sent and summed in bfloat16 or wider, within the bound.
No kernel may reach another device: no remote copies, remote signals or barrier semaphores. Data moves between devices by JAX's collectives and lax.ppermute only.
A program may use at most 64 MiB of HBM per device.

v0:
```python
import jax
import jax.numpy as jnp
from jax import lax
from jax.sharding import PartitionSpec as P


def layer_norm(values):
    center = values - jnp.mean(values, -1, keepdims=True)
    spread = jnp.mean(center * center, -1, keepdims=True)
    return center * lax.rsqrt(spread + 1e-05)


def edge_piece(edge_rows, sender_rows, receiver_rows, w_edge_in, w_edge_out):
    joined = jnp.concatenate(
        [edge_rows, sender_rows.astype(jnp.bfloat16), receiver_rows.astype(jnp.bfloat16)], 1
    )
    hidden = jax.nn.silu(jnp.dot(joined, w_edge_in, preferred_element_type=jnp.float32)).astype(
        jnp.bfloat16
    )
    update = layer_norm(jnp.dot(hidden, w_edge_out, preferred_element_type=jnp.float32))
    return (edge_rows.astype(jnp.float32) + update).astype(jnp.bfloat16)


def node_piece(mesh_wide, grid_sum, edge_sum, w_node_in, w_node_out):
    joined = jnp.concatenate(
        [
            mesh_wide.astype(jnp.bfloat16),
            grid_sum.astype(jnp.bfloat16),
            edge_sum.astype(jnp.bfloat16),
        ],
        1,
    )
    hidden = jax.nn.silu(jnp.dot(joined, w_node_in, preferred_element_type=jnp.float32)).astype(
        jnp.bfloat16
    )
    update = layer_norm(jnp.dot(hidden, w_node_out, preferred_element_type=jnp.float32))
    return (mesh_wide + update).astype(jnp.bfloat16)


def body(
    grid_latents,
    grid_region,
    grid_node,
    mesh_latents,
    edge_latents,
    edge_sender,
    edge_receiver,
    halo_send,
    w_grid,
    w_edge_in,
    w_edge_out,
    w_node_in,
    w_node_out,
    cot_mesh,
    cot_edges,
):
    spaces = lax.axis_size("space")
    feat_count = lax.axis_size("feat")
    feat_index = lax.axis_index("feat")
    node_rows, feat_width = mesh_latents.shape
    halo_block = halo_send.shape[2]
    capacity = max(2, 2 * grid_latents.shape[0] // spaces)
    share_rows = node_rows // feat_count
    node_index = jnp.arange(node_rows, dtype=jnp.int32)
    message = jax.nn.silu(jnp.dot(grid_latents, w_grid, preferred_element_type=jnp.float32)).astype(
        jnp.bfloat16
    )
    target_region = grid_region[:, 0]
    membership = (target_region[:, None] == jnp.arange(spaces, dtype=jnp.int32)[None, :]).astype(
        jnp.int32
    )
    earlier = jnp.cumsum(membership, 0) - membership
    placed = target_region * capacity + jnp.sum(earlier * membership, 1)
    outgoing = jnp.zeros((spaces * capacity, feat_width), jnp.bfloat16).at[placed].set(message)
    slot_labels = jnp.full((spaces * capacity,), -1, jnp.int32).at[placed].set(grid_node)
    arrived, arrived_labels = (
        lax.all_to_all(
            outgoing.reshape(spaces, capacity, feat_width),
            "space",
            split_axis=0,
            concat_axis=0,
            tiled=True,
        ),
        lax.all_to_all(
            slot_labels.reshape(spaces, capacity), "space", split_axis=0, concat_axis=0, tiled=True
        ),
    )
    grid_picker = (node_index[:, None] == arrived_labels.reshape(1, -1)).astype(jnp.bfloat16)
    grid_part = jnp.dot(
        grid_picker, arrived.reshape(-1, feat_width), preferred_element_type=jnp.float32
    )
    send_rows = halo_send[0]
    fetched = lax.all_to_all(
        mesh_latents[send_rows], "space", split_axis=0, concat_axis=0, tiled=True
    )
    mesh_wide = mesh_latents.astype(jnp.float32)
    lookup_table = jnp.concatenate(
        [mesh_wide, fetched.reshape(-1, feat_width).astype(jnp.float32)], 0
    )

    def edge_local(edge_rows, sender_rows, receiver_rows):
        return edge_piece(edge_rows, sender_rows, receiver_rows, w_edge_in, w_edge_out)

    new_edges, edge_back = jax.vjp(
        edge_local, edge_latents, lookup_table[edge_sender], mesh_wide[edge_receiver]
    )
    edge_picker = (node_index[:, None] == edge_receiver[None, :]).astype(jnp.bfloat16)
    edge_part = jnp.dot(edge_picker, new_edges, preferred_element_type=jnp.float32)
    grid_sum, edge_sum = (
        lax.psum(grid_part.astype(jnp.bfloat16), "feat").astype(jnp.float32),
        lax.psum(edge_part.astype(jnp.bfloat16), "feat").astype(jnp.float32),
    )

    def node_local(mesh_rows, edge_rows_sum):
        return node_piece(mesh_rows, grid_sum, edge_rows_sum, w_node_in, w_node_out)

    new_mesh, node_back = jax.vjp(node_local, mesh_wide, edge_sum)
    mesh_grad_all, edge_sum_grad = node_back(cot_mesh)
    mesh_grad_own = lax.dynamic_slice_in_dim(mesh_grad_all, feat_index * share_rows, share_rows, 0)
    edge_cot = cot_edges + edge_sum_grad[edge_receiver].astype(jnp.bfloat16)
    grad_edges, sender_grad, receiver_grad = edge_back(edge_cot)
    lookup_grad = jax.ops.segment_sum(sender_grad, edge_sender, num_segments=lookup_table.shape[0])
    local_grad = lookup_grad[:node_rows] + jax.ops.segment_sum(
        receiver_grad, edge_receiver, num_segments=node_rows
    )
    halo_grad = lookup_grad[node_rows:].reshape(spaces, halo_block, feat_width)
    returned = lax.all_to_all(
        halo_grad.astype(jnp.bfloat16), "space", split_axis=0, concat_axis=0, tiled=True
    ).astype(halo_grad.dtype)
    local_grad = local_grad + jax.ops.segment_sum(
        returned.reshape(-1, feat_width), send_rows.reshape(-1), num_segments=node_rows
    )
    grad_share = (
        lax.psum_scatter(
            local_grad.astype(jnp.bfloat16), "feat", scatter_dimension=0, tiled=True
        ).astype(jnp.float32)
        + mesh_grad_own
    )
    return (new_mesh, new_edges, grad_share.astype(jnp.bfloat16), grad_edges)


def solution(mesh):
    return jax.shard_map(
        body,
        mesh=mesh,
        in_specs=(
            P(("space", "feat"), None),
            P(("space", "feat"), None),
            P(("space", "feat")),
            P("space", None),
            P(("space", "feat"), None),
            P(("space", "feat")),
            P(("space", "feat")),
            P("space", None, None),
            P(),
            P(),
            P(),
            P(),
            P(),
            P("space", None),
            P(("space", "feat"), None),
        ),
        out_specs=(
            P("space", None),
            P(("space", "feat"), None),
            P(("space", "feat"), None),
            P(("space", "feat"), None),
        ),
        check_vma=False,
    )
```

profile of v0, /device:TPU:6, one launch (start us, length us, event | category | flops | bytes accessed | tf_op | source)
XLA Modules:
  0.0 345.8 jit_solution(17570173206879639572)
XLA Ops:
  7.2 0.8 fusion.56
  8.8 0.8 fusion.55
  9.6 0.7 compare_select_fusion.1
  10.3 1.6 scatter_custom_fusion
  11.9 0.7 all_to_all.15
  12.6 13.8 %all-to-all-start = ((s32[64,1,8]{2,1,0:T(1,128)}), s32[64,1,8]{2,1,0:T(1,128)S(1)}, u32[]{:S(2)}, u32[]{:S(2)}) async-start(s32[64,1,8]{2,1,0:T(1,128)} %bitcast.5), calls=%async_computation | async-start | bytes 65536 | tf_op jit(solution)/shard_map/all_to_all | solution.py:84
  26.4 1.5 fusion.74
  27.9 2.4 scatter_custom_fusion.1
  30.3 3.6 %all-to-all-done = s32[64,1,8]{2,1,0:T(1,128)S(1)} async-done(((s32[64,1,8]{2,1,0:T(1,128)}), s32[64,1,8]{2,1,0:T(1,128)S(1)}, u32[]{:S(2)}, u32[]{:S(2)}) %all-to-all-start) | async-done | bytes 2080 | tf_op jit(solution)/shard_map/all_to_all | solution.py:84
  33.9 6.8 %all-to-all-start.1 = ((bf16[64,8,512]{2,1,0:T(8,128)(2,1)}), bf16[64,8,512]{2,1,0:T(8,128)(2,1)S(1)}, u32[]{:S(2)}, u32[]{:S(2)}) async-start(bf16[64,8,512]{2,1,0:T(8,128)(2,1)} %bitcast.6), calls=%async_computation.1 | async-start | bytes 1048576 | tf_op jit(solution)/shard_map/all_to_all | solution.py:77
  40.9 2.7 gather_fusion
  43.6 1.2 reshape.135
  44.8 12.6 %all-to-all-done.1 = bf16[64,8,512]{2,1,0:T(8,128)(2,1)S(1)} async-done(((bf16[64,8,512]{2,1,0:T(8,128)(2,1)}), bf16[64,8,512]{2,1,0:T(8,128)(2,1)S(1)}, u32[]{:S(2)}, u32[]{:S(2)}) %all-to-all-start.1) | async-done | bytes 524320 | tf_op jit(solution)/shard_map/all_to_all | solution.py:77
  57.4 6.9 %all-to-all-start.2 = ((bf16[64,12,512]{2,1,0:T(8,128)(2,1)}), bf16[64,12,512]{2,1,0:T(8,128)(2,1)S(1)}, u32[]{:S(2)}, u32[]{:S(2)}) async-start(bf16[64,12,512]{2,1,0:T(8,128)(2,1)} %reshape.135), calls=%async_computation.2 | async-start | bytes 2097152 | tf_op jit(solution)/shard_map/all_to_all | solution.py:93
  64.6 2.6 gather_fusion.2
  67.7 0.7 reduce.5
  68.5 1.0 convolution_convert_fusion.4
  69.4 21.5 %all-to-all-done.2 = bf16[64,12,512]{2,1,0:T(8,128)(2,1)S(1)} async-done(((bf16[64,12,512]{2,1,0:T(8,128)(2,1)}), bf16[64,12,512]{2,1,0:T(8,128)(2,1)S(1)}, u32[]{:S(2)}, u32[]{:S(2)}) %all-to-all-start.2) | async-done | bytes 786464 | tf_op jit(solution)/shard_map/all_to_all | solution.py:93
  90.9 1.0 reshape.131
  92.0 1.2 pad_maximum_fusion
  93.2 2.1 gather_fusion.1
  95.3 1.8 fusion.1
  98.6 0.7 copy-done.6
  99.4 1.0 convolution_convert_fusion.3
  100.4 113.9 %all-reduce.3.cloned.1.call-done = (bf16[192,512]{1,0:T(8,128)(2,1)}, bf16[192,512]{1,0:T(8,128)(2,1)}) async-done(((bf16[192,512]{1,0:T(8,128)(2,1)}, bf16[192,512]{1,0:T(8,128)(2,1)}), (bf16[192,512]{1,0:T(8,128)(2,1)}, bf16[192,512]{1,0:T(8,128)(2,1)})) %all-reduce.3.cloned.1.call-update) | async-done | bytes 393232 | tf_op jit(solution)/shard_map/psum | solution.py:111
  214.3 2.1 fusion.21
  216.8 0.7 copy-done.4
  217.8 0.9 fusion.69
  218.7 3.5 convolution_convert_fusion.1
  222.1 1.7 fusion.71
  223.8 2.1 gather_fusion.3
  225.9 1.3 fusion.10
  227.9 3.6 %convolution_convert_fusion = bf16[384,1536]{1,0:T(8,128)(2,1)} fusion(bf16[1536,512]{1,0:T(8,128)(2,1)S(1)} %copy-done, f32[384,512]{1,0:T(8,128)} %copy-done.17, bf16[512,512]{1,0:T(8,128)(2,1)} %param.25, f32[384]{0:T(512)S(1)} %negate_multiply_fusion, bf16[384,512]{1,0:T(8,128)(2,1)S(1)} %get-tuple-element.9, f32[384,512]{1,0:T(8,128)S(1)} %get-tuple-element.17, ...), kind=kOutput, calls=%fused_computation.9 | convolution fusion | flops 809435136 | bytes 5249024 | tf_op jit(solution)/shard_map/transpose(jvp())/dot_general | solution.py:17
  231.5 3.8 %scatter_custom_fusion.2 = f32[960,512]{1,0:T(8,128)S(1)} fusion(s32[384]{0:T(512)} %param.20, f32[]{:T(128)} %constant.22.clone.1, bf16[384,1536]{1,0:T(8,128)(2,1)} %convolution_convert_fusion), kind=kCustom, calls=%fused_computation.29 | custom fusion | flops 393216 | bytes 2359808 | tf_op jit(solution)/shard_map/scatter-add | solution.py:122
  235.3 1.0 slice.30
  236.3 2.1 convert_element_type.134
  238.5 10.6 %all-to-all-start.3 = ((bf16[64,12,512]{2,1,0:T(8,128)(2,1)}), bf16[64,12,512]{2,1,0:T(8,128)(2,1)}, u32[]{:S(2)}, u32[]{:S(2)}) async-start(bf16[64,12,512]{2,1,0:T(8,128)(2,1)} %convert_element_type.134), calls=%async_computation.3 | async-start | bytes 2097152 | tf_op jit(solution)/shard_map/all_to_all | solution.py:127
  249.4 0.7 copy.25
  250.1 0.9 reshape.200
  251.0 0.8 slice.26
  251.7 5.0 %scatter_custom_fusion.3 = f32[192,512]{1,0:T(8,128)} fusion(f32[192,512]{1,0:T(8,128)} %slice.26, s32[384]{0:T(512)S(1)} %copy-done.12, bf16[384,1536]{1,0:T(8,128)(2,1)} %convolution_convert_fusion), kind=kCustom, calls=%fused_computation.34 | custom fusion | flops 393216 | bytes 786432 | tf_op jit(solution)/shard_map/scatter-add | solution.py:123
  256.8 18.9 %all-to-all-done.3 = bf16[64,12,512]{2,1,0:T(8,128)(2,1)} async-done(((bf16[64,12,512]{2,1,0:T(8,128)(2,1)}), bf16[64,12,512]{2,1,0:T(8,128)(2,1)}, u32[]{:S(2)}, u32[]{:S(2)}) %all-to-all-start.3) | async-done | bytes 786464 | tf_op jit(solution)/shard_map/all_to_all | solution.py:127
  275.7 2.3 reshape.202
  278.0 7.4 %scatter_custom_fusion.4 = f32[192,512]{1,0:T(8,128)S(1)} fusion(s32[768]{0:T(1024)S(1)} %reshape.200, f32[768,512]{1,0:T(8,128)} %reshape.202, f32[]{:T(128)} %constant.22.clone.1), kind=kCustom, calls=%fused_computation.79 | custom fusion | flops 393216 | bytes 393728 | tf_op jit(solution)/shard_map/scatter-add | solution.py:130
  285.4 0.7 add_convert_fusion.1
  286.3 1.8 slice_add_fusion
  288.0 49.6 %reduce-scatter.2.cloned.1.call-done = bf16[16,512]{1,0:T(8,128)(2,1)} async-done(((bf16[192,512]{1,0:T(8,128)(2,1)}), bf16[16,512]{1,0:T(8,128)(2,1)}) %reduce-scatter.2.cloned.1.call-update) | async-done | bytes 16400 | tf_op jit(solution)/shard_map/reduce_scatter | solution.py:134
  337.6 1.3 fusion.58
  (66 shorter events, 5.2 us)
Async XLA Ops:
  7.2 88.1 %copy-start = (bf16[1536,512]{1,0:T(8,128)(2,1)S(1)}, bf16[1536,512]{1,0:T(8,128)(2,1)}, u32[]{:S(2)}) copy-start(bf16[1536,512]{1,0:T(8,128)(2,1)} %param.24) | copy-start | bytes 4718596
  12.6 21.3 %all-to-all-start = ((s32[64,1,8]{2,1,0:T(1,128)}), s32[64,1,8]{2,1,0:T(1,128)S(1)}, u32[]{:S(2)}, u32[]{:S(2)}) async-start(s32[64,1,8]{2,1,0:T(1,128)} %bitcast.5), calls=%async_computation | async-start | bytes 65536 | tf_op jit(solution)/shard_map/all_to_all | solution.py:84
  26.4 14.3 %copy-start.10 = (s32[1,64,12]{1,0,2:T(1,128)S(1)}, s32[1,64,12]{1,0,2:T(1,128)}, u32[]{:S(2)}) copy-start(s32[1,64,12]{1,0,2:T(1,128)} %param.22) | copy-start | bytes 9220
  26.4 14.5 %copy-start.1 = (bf16[192,512]{1,0:T(8,128)(2,1)S(1)}, bf16[192,512]{1,0:T(8,128)(2,1)}, u32[]{:S(2)}) copy-start(bf16[192,512]{1,0:T(8,128)(2,1)} %param.18) | copy-start | bytes 589828
  33.9 23.5 %all-to-all-start.1 = ((bf16[64,8,512]{2,1,0:T(8,128)(2,1)}), bf16[64,8,512]{2,1,0:T(8,128)(2,1)S(1)}, u32[]{:S(2)}, u32[]{:S(2)}) async-start(bf16[64,8,512]{2,1,0:T(8,128)(2,1)} %bitcast.6), calls=%async_computation.1 | async-start | bytes 1048576 | tf_op jit(solution)/shard_map/all_to_all | solution.py:77
  43.6 20.9 %copy-start.11 = (s32[384]{0:T(512)S(1)}, s32[384]{0:T(512)}, u32[]{:S(2)}) copy-start(s32[384]{0:T(512)} %param.21) | copy-start | bytes 4612
  57.4 33.6 %all-to-all-start.2 = ((bf16[64,12,512]{2,1,0:T(8,128)(2,1)}), bf16[64,12,512]{2,1,0:T(8,128)(2,1)S(1)}, u32[]{:S(2)}, u32[]{:S(2)}) async-start(bf16[64,12,512]{2,1,0:T(8,128)(2,1)} %reshape.135), calls=%async_computation.2 | async-start | bytes 2097152 | tf_op jit(solution)/shard_map/all_to_all | solution.py:93
  64.3 150.0 %all-reduce.3.cloned.1.call-start = ((), (), s32[]{:S(2)}) async-start(), calls=%async_computation.6 | async-start | bytes 786432 | tf_op jit(solution)/shard_map/psum | solution.py:111
  64.5 2.6 copy-start.13
  93.2 2.1 copy-start.8
  95.3 1.8 copy-start.15
  97.1 0.9 copy-start.17
  97.1 1.3 copy-start.9
  98.0 1.4 copy-start.12
  98.6 0.7 copy-start.6
  214.3 2.1 copy-start.14
  216.4 2.2 copy-start.16
  216.4 1.1 copy-start.4
  227.1 0.8 copy-start.2
  238.5 37.2 %all-to-all-start.3 = ((bf16[64,12,512]{2,1,0:T(8,128)(2,1)}), bf16[64,12,512]{2,1,0:T(8,128)(2,1)}, u32[]{:S(2)}, u32[]{:S(2)}) async-start(bf16[64,12,512]{2,1,0:T(8,128)(2,1)} %convert_element_type.134), calls=%async_computation.3 | async-start | bytes 2097152 | tf_op jit(solution)/shard_map/all_to_all | solution.py:127
  249.1 88.5 %reduce-scatter.2.cloned.1.call-start = ((), (), s32[]{:S(2)}) async-start(), calls=%async_computation.5 | async-start | bytes 212992 | tf_op jit(solution)/shard_map/reduce_scatter | solution.py:134
  256.7 28.7 %copy-start.7 = (f32[192,512]{1,0:T(8,128)S(1)}, f32[192,512]{1,0:T(8,128)}, u32[]{:S(2)}) copy-start(f32[192,512]{1,0:T(8,128)} %scatter_custom_fusion.3) | copy-start | bytes 1179652
  256.8 29.4 %copy-start.5 = (bf16[192,512]{1,0:T(8,128)(2,1)S(1)}, bf16[192,512]{1,0:T(8,128)(2,1)}, u32[]{:S(2)}) copy-start(bf16[192,512]{1,0:T(8,128)(2,1)} %param.28) | copy-start | bytes 589828
  278.0 8.2 %copy-start.3 = (bf16[384,512]{1,0:T(8,128)(2,1)S(1)}, bf16[384,512]{1,0:T(8,128)(2,1)}, u32[]{:S(2)}) copy-start(bf16[384,512]{1,0:T(8,128)(2,1)} %copy-done.2) | copy-start | bytes 1179652
Sparse Core Ops, SparseCore 0:
  100.5 113.7 all-reduce.2
  286.3 51.2 reduce-scatter.1
where the time goes:
time: 347 us; the launch traced here: 346 us
  waiting for transfers between devices  220 us (63%)
  starting transfers between devices  38.6 us (11%)
  other arithmetic  30.6 us (9%)
  local copies, waits for them, and re-layouts  26.8 us (8%)
  matrix products  15.2 us (4%)
  between operations  14.5 us (4%)
    psum x1, waiting for transfers between devices, body(): lax.psum(edge_part.astype(jnp.bfloat16), 'feat').astype(jnp.float32)  114 us
    reduce_scatter x1, waiting for transfers between devices, body(): lax.psum_scatter(local_grad.astype(jnp.bfloat16), 'feat', scatter_dimensi...  49.6 us
    all_to_all x1, waiting for transfers between devices, body(): lax.all_to_all(mesh_latents[send_rows], 'space', split_axis=0, concat_axi...  21.5 us
    all_to_all x1, waiting for transfers between devices, body(): lax.all_to_all(halo_grad.astype(jnp.bfloat16), 'space', split_axis=0, con...  18.9 us
    all_to_all x1, starting transfers between devices, body(): lax.all_to_all(slot_labels.reshape(spaces, capacity), 'space', split_axis...  13.8 us
    all_to_all x1, waiting for transfers between devices, body(): lax.all_to_all(outgoing.reshape(spaces, capacity, feat_width), 'space', s...  12.6 us
    all_to_all x1, starting transfers between devices, body(): lax.all_to_all(halo_grad.astype(jnp.bfloat16), 'space', split_axis=0, con...  10.6 us
    scatter-add x1, other arithmetic, body(): jax.ops.segment_sum(returned.reshape(-1, feat_width), send_rows.reshape(-...  7.39 us
  transfers between devices with their start and end apart: 6, of which 6 were waited for; matrix products, arithmetic and copies ran while one was open for 6% of the time, Pallas kernels for 0%

commit v1 on v0

v1 whole, which is shorter than its diff:
```python
import functools

import jax
import jax.numpy as jnp
from jax import lax
from jax.experimental import pallas as pl
from jax.experimental.pallas import tpu as pltpu
from jax.sharding import PartitionSpec as P

BF = jnp.bfloat16
F32 = jnp.float32
VMEM_BYTES = 48 * 1024 * 1024


def mm(a, b):
    return jnp.dot(a, b, preferred_element_type=F32)


def mm_nt(a, b):
    return lax.dot_general(a, b, (((1,), (1,)), ((), ())), preferred_element_type=F32)


def iota(shape, dim):
    return lax.broadcasted_iota(jnp.int32, shape, dim)


def one_hot(a, b):
    return (a == b).astype(F32).astype(BF)


def column_of(row):
    n = row.shape[1]
    eye = iota((n, n), 0) == iota((n, n), 1)
    return jnp.sum(jnp.where(eye, row.astype(F32), 0.0), axis=1, keepdims=True).astype(jnp.int32)


def halo_column(halo_t, block, offset):
    count, spaces = halo_t.shape
    rows = spaces * 8
    spread = one_hot(iota((rows, spaces), 0) // 8, iota((rows, spaces), 1))
    all_k = mm_nt(spread, halo_t.astype(F32).astype(BF))
    wanted = offset + (iota((rows, count), 0) % 8) % block
    keep = wanted == iota((rows, count), 1)
    return jnp.sum(jnp.where(keep, all_k, 0.0), axis=1, keepdims=True).astype(jnp.int32)


def halo_row(halo_t, block, offset):
    count, spaces = halo_t.shape
    rows = spaces * 8
    spread = one_hot(iota((spaces, rows), 0), iota((spaces, rows), 1) // 8)
    all_k = mm(halo_t.astype(F32).astype(BF), spread)
    wanted = offset + (iota((count, rows), 1) % 8) % block
    keep = wanted == iota((count, rows), 0)
    return jnp.sum(jnp.where(keep, all_k, 0.0), axis=0, keepdims=True).astype(jnp.int32)


def silu_parts(v):
    s = 1.0 / (1.0 + jnp.exp(-v))
    return v * s, s * (1.0 + v * (1.0 - s))


def pack_kernel(grid_ref, w_ref, region_ref, node_ref, mesh_ref, halo_ref, out_ref):
    rows, width = grid_ref.shape
    half = width // 2
    spaces = halo_ref.shape[1]
    slots = spaces * 8
    v = mm(grid_ref[...], w_ref[...])
    message = silu_parts(v)[0].astype(BF)
    region = region_ref[...]
    member = one_hot(iota((spaces, rows), 0), region)
    before = (iota((rows, rows), 0) < iota((rows, rows), 1)).astype(F32).astype(BF)
    earlier = mm(member, before)
    rank = jnp.sum(earlier * member.astype(F32), axis=0, keepdims=True).astype(jnp.int32)
    slot = region * 8 + rank
    place = iota((slots, rows), 0) == slot
    labels = jnp.sum(
        jnp.where(place, (node_ref[...] + 1).astype(F32), 0.0), axis=1, keepdims=True
    )
    out_ref[:, width + half : 2 * width + half] = mm(
        place.astype(F32).astype(BF), message
    ).astype(BF)
    out_ref[:, 2 * width + half :] = jnp.broadcast_to(labels, (slots, 128)).astype(BF)
    mesh = mesh_ref[...]
    nodes = mesh.shape[0]
    halo_t = halo_ref[...]
    first = halo_column(halo_t, 8, 0)
    out_ref[:, :width] = mm(one_hot(first, iota((slots, nodes), 1)), mesh).astype(BF)
    rest = halo_column(halo_t, 4, 8)
    tail = mm(one_hot(rest, iota((slots, nodes), 1)), mesh)
    left = iota((slots, half), 0) % 8 < 4
    out_ref[:, width : width + half] = jnp.where(left, tail[:, :half], tail[:, half:]).astype(BF)


def table_ids(shape, dim, nodes, count):
    index = iota(shape, dim)
    peer = index // 8
    j = index % 8
    base = nodes + peer * count
    whole = base + j
    tail = base + 8 + j % 4
    return whole, jnp.where(j < 4, tail, -1), jnp.where(j < 4, -1, tail)


def edge_forward_kernel(
    got_ref,
    edge_ref,
    sender_ref,
    receiver_ref,
    mesh_ref,
    w_in_ref,
    w_out_ref,
    new_ref,
    sums_ref,
    slope_ref,
    xhat_ref,
    rstd_ref,
    count,
):
    edges, width = edge_ref.shape
    half = width // 2
    nodes = mesh_ref.shape[0]
    slots = got_ref.shape[0]
    feats = sums_ref.shape[0]
    share = nodes // feats
    mesh = mesh_ref[...]
    edge = edge_ref[...]
    sender = column_of(sender_ref[...])
    receiver = column_of(receiver_ref[...])
    whole, left, right = table_ids((1, slots), 1, nodes, count)
    head = mm(one_hot(sender, iota((edges, nodes), 1)), mesh) + mm(
        one_hot(sender, whole), got_ref[:, :width]
    )
    tail = got_ref[:, width : width + half]
    tail_left = mm(one_hot(sender, left), tail)
    tail_right = mm(one_hot(sender, right), tail)
    sender_rows = (head + jnp.concatenate([tail_left, tail_right], 1)).astype(BF)
    receiver_rows = mm(one_hot(receiver, iota((edges, nodes), 1)), mesh).astype(BF)
    v = (
        mm(edge, w_in_ref[:width, :])
        + mm(sender_rows, w_in_ref[width : 2 * width, :])
        + mm(receiver_rows, w_in_ref[2 * width :, :])
    )
    act, slope = silu_parts(v)
    slope_ref[...] = slope
    u = mm(act.astype(BF), w_out_ref[...])
    center = u - jnp.mean(u, -1, keepdims=True)
    rstd = lax.rsqrt(jnp.mean(center * center, -1, keepdims=True) + 1e-05)
    xhat = center * rstd
    xhat_ref[...] = xhat
    rstd_ref[...] = jnp.broadcast_to(rstd, rstd_ref.shape)
    new = (edge.astype(F32) + xhat).astype(BF)
    new_ref[...] = new
    edge_sum = mm(one_hot(iota((nodes, edges), 0), receiver_ref[...]), new).astype(BF)
    sums_ref[:, :, :width] = edge_sum.reshape(feats, share, width)
    label = got_ref[:, 2 * width + half :].astype(F32).T[0:1, :].astype(jnp.int32)
    grid_sum = mm(
        one_hot(iota((nodes, slots), 0) + 1, label), got_ref[:, width + half : 2 * width + half]
    ).astype(BF)
    sums_ref[:, :, width:] = grid_sum.reshape(feats, share, width)


def node_kernel(
    feat_ref,
    sums_ref,
    mesh_ref,
    cot_ref,
    w_in_ref,
    w_out_ref,
    new_ref,
    spread_ref,
    own_ref,
):
    feats, share, both = sums_ref.shape
    width = both // 2
    start = pl.multiple_of(feat_ref[0] * share, share)
    mesh = mesh_ref[pl.ds(start, share), :]
    cot = cot_ref[pl.ds(start, share), :].astype(F32)
    sums = jnp.sum(sums_ref[...].astype(F32), axis=0)
    edge_sum = sums[:, :width].astype(BF)
    grid_sum = sums[:, width:].astype(BF)
    v = (
        mm(mesh, w_in_ref[:width, :])
        + mm(grid_sum, w_in_ref[width : 2 * width, :])
        + mm(edge_sum, w_in_ref[2 * width :, :])
    )
    act, slope = silu_parts(v)
    u = mm(act.astype(BF), w_out_ref[...])
    center = u - jnp.mean(u, -1, keepdims=True)
    rstd = lax.rsqrt(jnp.mean(center * center, -1, keepdims=True) + 1e-05)
    xhat = center * rstd
    new_ref[...] = (mesh.astype(F32) + xhat).astype(BF)
    du = norm_back(cot, xhat, rstd)
    dh = mm_nt(du.astype(BF), w_out_ref[...]).astype(BF)
    dv = (dh.astype(F32) * slope).astype(BF)
    sum_grad = mm_nt(dv, w_in_ref[2 * width :, :]).astype(BF)
    spread_ref[...] = jnp.broadcast_to(sum_grad[None], spread_ref.shape)
    own_ref[...] = cot + mm_nt(dv, w_in_ref[:width, :]).astype(BF).astype(F32)


def norm_back(cot, xhat, rstd):
    return rstd * (
        cot
        - jnp.mean(cot, -1, keepdims=True)
        - xhat * jnp.mean(cot * xhat, -1, keepdims=True)
    )


def edge_back_kernel(
    grads_ref,
    cot_ref,
    sender_ref,
    receiver_ref,
    slope_ref,
    xhat_ref,
    rstd_ref,
    w_in_ref,
    w_out_ref,
    new_ref,
    send_ref,
    edge_cot_ref,
    dv_ref,
    sgrad_ref,
    new_again_ref,
    nodes,
    count,
):
    new_again_ref[...] = new_ref[...]
    edges, width = cot_ref.shape
    half = width // 2
    slots = send_ref.shape[0]
    receiver = column_of(receiver_ref[...])
    spread = mm(one_hot(receiver, iota((edges, nodes), 1)), grads_ref[...])
    cot = (cot_ref[...].astype(F32) + spread).astype(BF)
    edge_cot_ref[...] = cot
    du = norm_back(cot.astype(F32), xhat_ref[...], rstd_ref[:, 0:1])
    dh = mm_nt(du.astype(BF), w_out_ref[...]).astype(BF)
    dv = (dh.astype(F32) * slope_ref[...]).astype(BF)
    dv_ref[...] = dv
    sgrad = mm_nt(dv, w_in_ref[width : 2 * width, :]).astype(BF)
    sgrad_ref[...] = sgrad
    whole, left, right = table_ids((slots, 1), 0, nodes, count)
    sender = sender_ref[...]
    send_ref[:, :width] = mm(one_hot(whole, sender), sgrad).astype(BF)
    tail = mm(one_hot(jnp.maximum(left, right), sender), sgrad)
    send_ref[:, width:] = jnp.where(left >= 0, tail[:, :half], tail[:, half:]).astype(BF)


def edge_rest_kernel(
    edge_cot_ref, dv_ref, sgrad_ref, sender_ref, receiver_ref, w_in_ref, grad_ref, local_ref
):
    edges, width = dv_ref.shape
    nodes = local_ref.shape[0]
    dv = dv_ref[...]
    direct = mm_nt(dv, w_in_ref[:width, :]).astype(BF)
    grad_ref[...] = (edge_cot_ref[...].astype(F32) + direct.astype(F32)).astype(BF)
    rgrad = mm_nt(dv, w_in_ref[2 * width :, :]).astype(BF)
    ids = iota((nodes, edges), 0)
    local_ref[...] = mm(one_hot(ids, sender_ref[...]), sgrad_ref[...]) + mm(
        one_hot(ids, receiver_ref[...]), rgrad
    )


def return_kernel(got_ref, local_ref, halo_ref, new_ref, out_ref, new_out_ref):
    new_out_ref[...] = new_ref[...]
    nodes, width = local_ref.shape
    half = width // 2
    slots = got_ref.shape[0]
    feats, share, _ = out_ref.shape
    halo_t = halo_ref[...]
    ids = iota((nodes, slots), 0)
    total = local_ref[...] + mm(one_hot(ids, halo_row(halo_t, 8, 0)), got_ref[:, :width])
    rest = halo_row(halo_t, 4, 8)
    is_left = iota((1, slots), 1) % 8 < 4
    tail = got_ref[:, width:]
    tail_left = mm(one_hot(ids, jnp.where(is_left, rest, -1)), tail)
    tail_right = mm(one_hot(ids, jnp.where(is_left, -1, rest)), tail)
    total = total + jnp.concatenate([tail_left, tail_right], 1)
    out_ref[...] = total.astype(BF).reshape(feats, share, width)


def finish_kernel(got_ref, own_ref, out_ref):
    out_ref[...] = (jnp.sum(got_ref[...].astype(F32), axis=0) + own_ref[...]).astype(BF)


def call(kernel, outs, args, smem=0):
    vmem = pl.BlockSpec(memory_space=pltpu.VMEM)
    return pl.pallas_call(
        kernel,
        out_shape=[jax.ShapeDtypeStruct(shape, dtype) for shape, dtype in outs],
        in_specs=[pl.BlockSpec(memory_space=pltpu.SMEM)] * smem + [vmem] * (len(args) - smem),
        out_specs=[vmem] * len(outs),
        compiler_params=pltpu.CompilerParams(vmem_limit_bytes=VMEM_BYTES),
    )(*args)


def swap(values, axis):
    return lax.all_to_all(values, axis, split_axis=0, concat_axis=0, tiled=True)


def body(
    grid_latents,
    grid_region,
    grid_node,
    mesh_latents,
    edge_latents,
    edge_sender,
    edge_receiver,
    halo_send,
    w_grid,
    w_edge_in,
    w_edge_out,
    w_node_in,
    w_node_out,
    cot_mesh,
    cot_edges,
):
    spaces = lax.axis_size("space")
    feats = lax.axis_size("feat")
    feat = lax.axis_index("feat").astype(jnp.int32).reshape(1)
    nodes, width = mesh_latents.shape
    edges = edge_latents.shape[0]
    count = halo_send.shape[2]
    share = nodes // feats
    slots = spaces * 8
    wide = 2 * width + width // 2 + 128
    back = width + width // 2
    region_row = grid_region.reshape(1, -1)
    node_row = grid_node.reshape(1, -1)
    sender = edge_sender.reshape(1, -1)
    receiver = edge_receiver.reshape(1, -1)
    halo_t = halo_send[0].T

    (packed,) = call(
        pack_kernel,
        [((slots, wide), BF)],
        (grid_latents, w_grid, region_row, node_row, mesh_latents, halo_t),
    )
    got = swap(packed.reshape(spaces, 8, wide), "space").reshape(slots, wide)
    new_edges, sums, slope, xhat, rstd = call(
        functools.partial(edge_forward_kernel, count=count),
        [
            ((edges, width), BF),
            ((feats, share, 2 * width), BF),
            ((edges, width), F32),
            ((edges, width), F32),
            ((edges, 128), F32),
        ],
        (got, edge_latents, sender, receiver, mesh_latents, w_edge_in, w_edge_out),
    )
    sums = swap(sums, "feat")
    new_share, spread, own = call(
        node_kernel,
        [((share, width), BF), ((feats, share, width), BF), ((share, width), F32)],
        (feat, sums, mesh_latents, cot_mesh, w_node_in, w_node_out),
        smem=1,
    )
    grads = swap(spread, "feat").reshape(nodes, width)
    send, edge_cot, dv, sgrad, new_share = call(
        functools.partial(edge_back_kernel, nodes=nodes, count=count),
        [
            ((slots, back), BF),
            ((edges, width), BF),
            ((edges, width), BF),
            ((edges, width), BF),
            ((share, width), BF),
        ],
        (grads, cot_edges, sender, receiver, slope, xhat, rstd, w_edge_in, w_edge_out, new_share),
    )
    returned = swap(send.reshape(spaces, 8, back), "space").reshape(slots, back)
    grad_edges, local = call(
        edge_rest_kernel,
        [((edges, width), BF), ((nodes, width), F32)],
        (edge_cot, dv, sgrad, sender, receiver, w_edge_in),
    )
    new_mesh = lax.all_gather(new_share, "feat", axis=0, tiled=True)
    parts, new_mesh = call(
        return_kernel,
        [((feats, share, width), BF), ((nodes, width), BF)],
        (returned, local, halo_t, new_mesh),
    )
    (grad_mesh,) = call(finish_kernel, [((share, width), BF)], (swap(parts, "feat"), own))
    return new_mesh, new_edges, grad_mesh, grad_edges


def solution(mesh):
    return jax.shard_map(
        body,
        mesh=mesh,
        in_specs=(
            P(("space", "feat"), None),
            P(("space", "feat"), None),
            P(("space", "feat")),
            P("space", None),
            P(("space", "feat"), None),
            P(("space", "feat")),
            P(("space", "feat")),
            P("space", None, None),
            P(),
            P(),
            P(),
            P(),
            P(),
            P("space", None),
            P(("space", "feat"), None),
        ),
        out_specs=(
            P("space", None),
            P(("space", "feat"), None),
            P(("space", "feat"), None),
            P(("space", "feat"), None),
        ),
        check_vma=False,
    )
```

time: 347 us -> 174 us (0.50)
  waiting for transfers between devices: 220 us -> 54.1 us
  blocking collectives: 0 us -> 57.8 us
  other arithmetic: 30.6 us -> 0 us
  matrix products: 15.2 us -> 0 us
  Pallas kernels: 0 us -> 15.2 us
  local copies, waits for them, and re-layouts: 26.8 us -> 12.4 us
  between operations: 14.5 us -> 0.75 us
  starting transfers between devices: 38.6 us -> 33.1 us
    psum x1 -> x0, waiting for transfers between devices: 114 us -> none  [body(): lax.psum(edge_part.astype(jnp.bfloat16), 'feat').astype(jnp.float32)]
    reduce_scatter x1 -> x0, waiting for transfers between devices: 49.6 us -> none  [body(): lax.psum_scatter(local_grad.astype(jnp.bfloat16), 'feat', scatter_dimensi...]
    all_to_all x0 -> x2, blocking collectives: none -> 35.5 us  [swap(): return lax.all_to_all(values, axis, split_axis=0, concat_axis=0, tiled=True)]
    all_gather x0 -> x1, blocking collectives: none -> 22.3 us  [body(): new_mesh = lax.all_gather(new_share, 'feat', axis=0, tiled=True)]
    scatter-add x3 -> x0, other arithmetic: 16.2 us -> none  [the longest x1 7.39 us: body(): jax.ops.segment_sum(returned.reshape(-1, feat_width), send_rows.reshape(-...]
    pallas_call x0 -> x7, Pallas kernels: none -> 15.2 us  [call(): pl.pallas_call(kernel, out_shape=[jax.ShapeDtypeStruct(shape, dtype) for...]
    dot_general x9 -> x0, matrix products: 15.2 us -> none  [the longest x2 5.59 us: node_piece(): jnp.dot(joined, w_node_in, preferred_element_type=jnp.float32)]
    gather x5 -> x0, local copies, waits for them, and re-layouts: 10.5 us -> none  [the longest x2 3.84 us: body(): mesh_latents[send_rows]]
  transfers between devices with their start and end apart: 6 -> 3, of which waited for: 6 -> 2; matrix products, arithmetic and copies ran while one was open for 6% -> 0% of each run, Pallas kernels for 0% -> 1%
where the time goes in v1:
time: 174 us; the launch traced here: 173 us
  blocking collectives  57.8 us (33%)
  waiting for transfers between devices  54.1 us (31%)
  starting transfers between devices  33.1 us (19%)
  Pallas kernels  15.2 us (9%)
  local copies, waits for them, and re-layouts  12.4 us (7%)
    all_to_all x3, waiting for transfers between devices, swap(): return lax.all_to_all(values, axis, split_axis=0, concat_axis=0, tiled=True)  54.1 us
    all_to_all x2, blocking collectives, swap(): return lax.all_to_all(values, axis, split_axis=0, concat_axis=0, tiled=True)  35.5 us
    all_to_all x3, starting transfers between devices, swap(): return lax.all_to_all(values, axis, split_axis=0, concat_axis=0, tiled=True)  33.1 us
    all_gather x1, blocking collectives, body(): new_mesh = lax.all_gather(new_share, 'feat', axis=0, tiled=True)  22.3 us
    pallas_call x7, Pallas kernels, call(): pl.pallas_call(kernel, out_shape=[jax.ShapeDtypeStruct(shape, dtype) for...  15.2 us
    unnamed x53, local copies, waits for them, and re-layouts  12.4 us
  transfers between devices with their start and end apart: 3, of which 2 were waited for; matrix products, arithmetic and copies ran while one was open for 0% of the time, Pallas kernels for 1%

profile of v1, /device:TPU:6, one launch (start us, length us, event | category | flops | bytes accessed | tf_op | source)
XLA Modules:
  0.0 173.4 jit_solution(10127238315861653506)
XLA Ops:
  0.6 0.7 copy.21
  1.3 0.0 copy-start.2
  1.3 0.9 copy-done.2
  2.3 0.0 copy-start.7
  2.3 1.0 copy-done.7
  3.3 0.0 copy-start.14
  3.3 0.9 copy-done.14
  4.2 0.0 copy-start.22
  4.2 0.7 copy-done.22
  4.9 0.7 copy-done.23
  5.6 2.3 %shard_map.174 = bf16[512,1408]{1,0:T(8,128)(2,1)} custom-call(bf16[256,512]{1,0:T(8,128)(2,1)S(1)} %copy-done.14, bf16[512,512]{1,0:T(8,128)(2,1)S(1)} %copy-done.7, s32[1,256]{1,0:T(1,128)S(1)} %bitcast.18, s32[1,256]{1,0:T(1,128)S(1)} %bitcast.19, bf16[192,512]{1,0:T(8,128)(2,1)S(1)} %copy-done.2, s32[12,64]{1,0:T(8,128)S(1)} %bitcast.16), custom_call_target="tpu_custom_call" | custom-call | tf_op jit(solution)/shard_map/pallas_call | solution.py:287
  7.9 14.1 %all-to-all-start = ((bf16[64,8,1408]{2,1,0:T(8,128)(2,1)}), bf16[64,8,1408]{2,1,0:T(8,128)(2,1)S(1)}, u32[]{:S(2)}, u32[]{:S(2)}) async-start(bf16[64,8,1408]{2,1,0:T(8,128)(2,1)} %bitcast.4), calls=%async_computation | async-start | bytes 2883584 | tf_op jit(solution)/shard_map/all_to_all | solution.py:297
  22.0 0.0 copy-done.24
  22.0 0.0 copy-done.25
  22.1 34.9 %all-to-all-done = bf16[64,8,1408]{2,1,0:T(8,128)(2,1)S(1)} async-done(((bf16[64,8,1408]{2,1,0:T(8,128)(2,1)}), bf16[64,8,1408]{2,1,0:T(8,128)(2,1)S(1)}, u32[]{:S(2)}, u32[]{:S(2)}) %all-to-all-start) | async-done | bytes 1441824 | tf_op jit(solution)/shard_map/all_to_all | solution.py:297
  56.9 0.0 copy-done.1
  56.9 0.0 copy-done.3
  56.9 1.0 copy-done.9
  57.9 4.4 %shard_map.175 = (bf16[384,512]{1,0:T(8,128)(2,1)}, bf16[12,16,1024]{2,1,0:T(8,128)(2,1)S(1)}, f32[384,512]{1,0:T(8,128)S(1)}, f32[384,512]{1,0:T(8,128)S(1)}, f32[384,128]{1,0:T(8,128)S(1)}) custom-call(bf16[512,1408]{1,0:T(8,128)(2,1)S(1)} %bitcast.13, bf16[384,512]{1,0:T(8,128)(2,1)S(1)} %copy-done.9, s32[1,384]{1,0:T(1,128)S(1)} %reshape.43.sender_ref, ...), custom_call_target="tpu_custom_call" | custom-call | tf_op jit(solution)/shard_map/pallas_call | solution.py:287
  62.3 0.9 copy-done.5
  63.2 0.7 copy-done.11
  64.0 0.7 copy-done.15
  64.6 12.1 %all-to-all-start.1 = ((bf16[12,16,1024]{2,1,0:T(8,128)(2,1)}), bf16[12,16,1024]{2,1,0:T(8,128)(2,1)S(1)}, u32[]{:S(2)}, u32[]{:S(2)}) async-start(bf16[12,16,1024]{2,1,0:T(8,128)(2,1)} %copy-done.11), calls=%async_computation.1 | async-start | bytes 786432 | tf_op jit(solution)/shard_map/all_to_all | solution.py:297
  76.7 19.3 %all-to-all-done.1.sums_ref = bf16[12,16,1024]{2,1,0:T(8,128)(2,1)S(1)} async-done(((bf16[12,16,1024]{2,1,0:T(8,128)(2,1)}), bf16[12,16,1024]{2,1,0:T(8,128)(2,1)S(1)}, u32[]{:S(2)}, u32[]{:S(2)}) %all-to-all-start.1) | async-done | bytes 393248 | tf_op jit(solution)/shard_map/all_to_all | solution.py:297
  96.0 0.0 copy-done.8
  96.0 1.4 copy-done.4
  97.4 0.9 copy-done.17
  98.3 1.2 shard_map.176
  99.6 19.2 %all_to_all.25 = bf16[12,16,512]{2,1,0:T(8,128)(2,1)S(1)} all-to-all(bf16[12,16,512]{2,1,0:T(8,128)(2,1)S(1)} %get-tuple-element.22), channel_id=1, replica_groups=mesh['space'=64,'feat'=12] {'feat'}, dimensions={0} | all-to-all | bytes 393216 | tf_op jit(solution)/shard_map/all_to_all | solution.py:297
  118.8 0.0 copy-done.6
  118.8 0.0 copy-done.10
  118.8 0.0 copy-done.16
  118.8 4.1 %shard_map.177 = (bf16[512,768]{1,0:T(8,128)(2,1)}, bf16[384,512]{1,0:T(8,128)(2,1)S(1)}, bf16[384,512]{1,0:T(8,128)(2,1)S(1)}, bf16[384,512]{1,0:T(8,128)(2,1)S(1)}, bf16[16,512]{1,0:T(8,128)(2,1)S(1)}) custom-call(bf16[192,512]{1,0:T(8,128)(2,1)S(1)} %bitcast.15, bf16[384,512]{1,0:T(8,128)(2,1)S(1)} %copy-done.10, s32[1,384]{1,0:T(1,128)S(1)} %reshape.43.sender_ref, ...), custom_call_target="tpu_custom_call" | custom-call | tf_op jit(solution)/shard_map/pallas_call | solution.py:287
  122.9 0.0 copy-done.18
  122.9 0.7 copy-done.12
  123.6 7.0 %all-to-all-start.3 = ((bf16[64,8,768]{2,1,0:T(8,128)(2,1)}), bf16[64,8,768]{2,1,0:T(8,128)(2,1)S(1)}, u32[]{:S(2)}, u32[]{:S(2)}) async-start(bf16[64,8,768]{2,1,0:T(8,128)(2,1)} %bitcast.7), calls=%async_computation.3 | async-start | bytes 1572864 | tf_op jit(solution)/shard_map/all_to_all | solution.py:297
  130.7 0.0 copy-done.20
  130.7 0.0 copy-done
  130.7 0.0 copy-start.13
  130.7 1.0 copy-done.13
  131.7 1.5 shard_map.178
  133.2 0.0 copy-done.21
  133.2 22.3 %all_gather.3.new_ref = bf16[192,512]{1,0:T(8,128)(2,1)S(1)} all-gather(bf16[16,512]{1,0:T(8,128)(2,1)S(1)} %copy-done.21), channel_id=1, replica_groups=mesh['space'=64,'feat'=12] {'feat'}, dimensions={0}, use_global_device_ids=true | all-gather | bytes 212992 | tf_op jit(solution)/shard_map/all_gather | solution.py:375
  155.5 0.0 all-to-all-done.3
  155.5 1.1 shard_map.179
  156.5 16.3 %all_to_all.26.got_ref = bf16[12,16,512]{2,1,0:T(8,128)(2,1)S(1)} all-to-all(bf16[12,16,512]{2,1,0:T(8,128)(2,1)S(1)} %get-tuple-element.35), channel_id=1, replica_groups=mesh['space'=64,'feat'=12] {'feat'}, dimensions={0} | all-to-all | bytes 393216 | tf_op jit(solution)/shard_map/all_to_all | solution.py:297
  172.8 0.0 copy-done.19
  172.8 0.6 shard_map.180
  (23 shorter events, 0.0 us)
Async XLA Ops:
  1.3 0.9 copy-start.2
  2.3 1.0 copy-start.7
  3.3 0.9 copy-start.14
  4.2 0.7 copy-start.22
  4.9 0.7 copy-start.23
  7.9 14.1 %copy-start.24 = (s32[384]{0:T(512)S(1)}, s32[384]{0:T(512)}, u32[]{:S(2)}) copy-start(s32[384]{0:T(512)} %param.20) | copy-start | bytes 4612
  7.9 14.1 %copy-start.25 = (s32[384]{0:T(512)S(1)}, s32[384]{0:T(512)}, u32[]{:S(2)}) copy-start(s32[384]{0:T(512)} %param.21) | copy-start | bytes 4612
  7.9 49.0 %copy-start.1 = (bf16[512,512]{1,0:T(8,128)(2,1)S(1)}, bf16[512,512]{1,0:T(8,128)(2,1)}, u32[]{:S(2)}) copy-start(bf16[512,512]{1,0:T(8,128)(2,1)} %w_out_ref.5) | copy-start | bytes 1572868
  7.9 49.0 %copy-start.3 = (bf16[192,512]{1,0:T(8,128)(2,1)S(1)}, bf16[192,512]{1,0:T(8,128)(2,1)}, u32[]{:S(2)}) copy-start(bf16[192,512]{1,0:T(8,128)(2,1)} %mesh_ref.5) | copy-start | bytes 589828
  7.9 49.0 %all-to-all-start = ((bf16[64,8,1408]{2,1,0:T(8,128)(2,1)}), bf16[64,8,1408]{2,1,0:T(8,128)(2,1)S(1)}, u32[]{:S(2)}, u32[]{:S(2)}) async-start(bf16[64,8,1408]{2,1,0:T(8,128)(2,1)} %bitcast.4), calls=%async_computation | async-start | bytes 2883584 | tf_op jit(solution)/shard_map/all_to_all | solution.py:297
  56.9 1.0 copy-start.9
  57.9 38.1 %copy-start.8 = (bf16[512,512]{1,0:T(8,128)(2,1)S(1)}, bf16[512,512]{1,0:T(8,128)(2,1)}, u32[]{:S(2)}) copy-start(bf16[512,512]{1,0:T(8,128)(2,1)} %w_out_ref.4) | copy-start | bytes 1572868
  62.3 0.9 copy-start.5
  63.2 0.7 copy-start.11
  64.0 0.7 copy-start.15
  64.6 31.3 %all-to-all-start.1 = ((bf16[12,16,1024]{2,1,0:T(8,128)(2,1)}), bf16[12,16,1024]{2,1,0:T(8,128)(2,1)S(1)}, u32[]{:S(2)}, u32[]{:S(2)}) async-start(bf16[12,16,1024]{2,1,0:T(8,128)(2,1)} %copy-done.11), calls=%async_computation.1 | async-start | bytes 786432 | tf_op jit(solution)/shard_map/all_to_all | solution.py:297
  96.0 1.4 copy-start.4
  97.4 0.9 copy-start.17
  98.3 20.5 %copy-start.6 = (f32[384,512]{1,0:T(8,128)S(1)}, f32[384,512]{1,0:T(8,128)}, u32[]{:S(2)}) copy-start(f32[384,512]{1,0:T(8,128)} %copy-done.5) | copy-start | bytes 2359300
  98.3 20.5 %copy-start.10 = (bf16[384,512]{1,0:T(8,128)(2,1)S(1)}, bf16[384,512]{1,0:T(8,128)(2,1)}, u32[]{:S(2)}) copy-start(bf16[384,512]{1,0:T(8,128)(2,1)} %cot_ref.3) | copy-start | bytes 1179652
  98.3 20.5 %copy-start.16 = (f32[384,128]{1,0:T(8,128)S(1)}, f32[384,128]{1,0:T(8,128)}, u32[]{:S(2)}) copy-start(f32[384,128]{1,0:T(8,128)} %copy-done.15) | copy-start | bytes 589828
  99.6 23.3 %copy-start.18 = (f32[16,512]{1,0:T(8,128)}, f32[16,512]{1,0:T(8,128)S(1)}, u32[]{:S(2)}) copy-start(f32[16,512]{1,0:T(8,128)S(1)} %get-tuple-element.36.own_ref) | copy-start | bytes 98308
  122.9 0.7 copy-start.12
  123.6 7.0 %copy-start.20 = (bf16[16,512]{1,0:T(8,128)(2,1)}, bf16[16,512]{1,0:T(8,128)(2,1)S(1)}, u32[]{:S(2)}) copy-start(bf16[16,512]{1,0:T(8,128)(2,1)S(1)} %get-tuple-element.32) | copy-start | bytes 49156
  123.6 7.0 %copy-start = (bf16[1536,512]{1,0:T(8,128)(2,1)S(1)}, bf16[1536,512]{1,0:T(8,128)(2,1)}, u32[]{:S(2)}) copy-start(bf16[1536,512]{1,0:T(8,128)(2,1)} %w_in_ref.7) | copy-start | bytes 4718596
  123.6 31.9 %all-to-all-start.3 = ((bf16[64,8,768]{2,1,0:T(8,128)(2,1)}), bf16[64,8,768]{2,1,0:T(8,128)(2,1)S(1)}, u32[]{:S(2)}, u32[]{:S(2)}) async-start(bf16[64,8,768]{2,1,0:T(8,128)(2,1)} %bitcast.7), calls=%async_computation.3 | async-start | bytes 1572864 | tf_op jit(solution)/shard_map/all_to_all | solution.py:297
  130.7 1.0 copy-start.13
  131.7 1.5 copy-start.21
  133.2 39.6 %copy-start.19 = (f32[16,512]{1,0:T(8,128)S(1)}, f32[16,512]{1,0:T(8,128)}, u32[]{:S(2)}) copy-start(f32[16,512]{1,0:T(8,128)} %copy-done.18) | copy-start | bytes 98308

commit v2 on v1

v2 whole, which is shorter than its diff:
```python
import functools

import jax
import jax.numpy as jnp
from jax import lax
from jax.experimental import pallas as pl
from jax.experimental.pallas import tpu as pltpu
from jax.sharding import PartitionSpec as P

BF = jnp.bfloat16
F32 = jnp.float32
VMEM_BYTES = 20 * 1024 * 1024


def mm(a, b):
    return jnp.dot(a, b, preferred_element_type=F32)


def mm_nt(a, b):
    return lax.dot_general(a, b, (((1,), (1,)), ((), ())), preferred_element_type=F32)


def iota(shape, dim):
    return lax.broadcasted_iota(jnp.int32, shape, dim)


def one_hot(a, b):
    return (a == b).astype(F32).astype(BF)


def column_of(row):
    n = row.shape[1]
    eye = iota((n, n), 0) == iota((n, n), 1)
    return jnp.sum(jnp.where(eye, row.astype(F32), 0.0), axis=1, keepdims=True).astype(jnp.int32)


class Fetch:
    def __init__(self, array, rows=None, start=None, keep=False):
        self.array, self.start, self.keep = array, start, keep
        self.shape = array.shape if rows is None else (rows,) + array.shape[1:]

    def source(self, ref):
        if self.start is None:
            return ref
        return ref.at[pl.ds(self.start() if callable(self.start) else self.start, self.shape[0])]


class Push:
    def __init__(self, shape, dtype):
        self.shape, self.dtype = shape, dtype


class Late:
    def __init__(self, source, target, sem):
        self.ref, self.shape, self.waited = target, target.shape, False
        self.copy = pltpu.make_async_copy(source, target, sem)
        self.copy.start()

    def wait(self):
        if not self.waited:
            self.copy.wait()
            self.waited = True

    def __getitem__(self, index):
        self.wait()
        return self.ref[index]


class Out:
    def __init__(self, target, scratch, sems):
        self.target, self.ref, self.sems, self.copies = target, scratch, sems, []
        self.shape = scratch.shape

    def put(self, value, *columns):
        source, target = self.ref, self.target
        if columns:
            index = (slice(None),) * (len(self.shape) - 1) + (slice(*columns),)
            self.ref[index] = value
            source, target = source.at[index], target.at[index]
        else:
            self.ref[...] = value
        copy = pltpu.make_async_copy(source, target, next(self.sems))
        copy.start()
        self.copies.append(copy)

    def wait(self):
        for copy in self.copies:
            copy.wait()


def call(kernel, outs, args):
    fetches = [arg for arg in args if isinstance(arg, Fetch)]
    kept = [arg for arg in fetches if arg.keep]
    pushes = [out for out in outs if isinstance(out, Push)]
    semaphores = len(fetches) + 4 * len(pushes)

    def run(*refs):
        ins, refs = refs[: len(args)], refs[len(args) :]
        plain_outs, refs = refs[: len(outs)], refs[len(outs) :]
        kept_refs, refs = iter(refs[: len(kept)]), refs[len(kept) :]
        scratch = iter(refs)
        sems = iter([refs[-1].at[i] for i in range(semaphores)] if semaphores else [])
        given = []
        for arg, ref in zip(args, ins):
            if isinstance(arg, Fetch):
                target = next(kept_refs if arg.keep else scratch)
                ref = Late(arg.source(ref), target, next(sems))
            given.append(ref)
        for out, ref in zip(outs, plain_outs):
            given.append(Out(ref, next(scratch), sems) if isinstance(out, Push) else ref)
        kernel(*given)
        for ref in given:
            if isinstance(ref, (Late, Out)):
                ref.wait()

    vmem = pl.BlockSpec(memory_space=pltpu.VMEM)
    hbm = pl.BlockSpec(memory_space=pltpu.HBM)
    scratch = [pltpu.VMEM(arg.shape, arg.array.dtype) for arg in fetches if not arg.keep]
    scratch += [pltpu.VMEM(out.shape, out.dtype) for out in pushes]
    if semaphores:
        scratch.append(pltpu.SemaphoreType.DMA((semaphores,)))
    out_shape = [
        pltpu.HBM(out.shape, out.dtype) if isinstance(out, Push) else pltpu.VMEM(*out)
        for out in outs
    ]
    results = pl.pallas_call(
        run,
        out_shape=out_shape + [pltpu.VMEM(arg.shape, arg.array.dtype) for arg in kept],
        in_specs=[hbm if isinstance(arg, Fetch) else vmem for arg in args],
        out_specs=[hbm if isinstance(out, Push) else vmem for out in outs] + [vmem] * len(kept),
        scratch_shapes=scratch,
        compiler_params=pltpu.CompilerParams(vmem_limit_bytes=VMEM_BYTES),
    )(
        *[
            pltpu.with_memory_space_constraint(arg.array, pltpu.HBM)
            if isinstance(arg, Fetch)
            else arg
            for arg in args
        ]
    )
    return results


def halo_column(halo_t, block, offset):
    count, spaces = halo_t.shape
    rows = spaces * 8
    spread = one_hot(iota((rows, spaces), 0) // 8, iota((rows, spaces), 1))
    all_k = mm_nt(spread, halo_t.astype(F32).astype(BF))
    wanted = offset + (iota((rows, count), 0) % 8) % block
    keep = wanted == iota((rows, count), 1)
    return jnp.sum(jnp.where(keep, all_k, 0.0), axis=1, keepdims=True).astype(jnp.int32)


def halo_row(halo_t, block, offset):
    count, spaces = halo_t.shape
    rows = spaces * 8
    spread = one_hot(iota((spaces, rows), 0), iota((spaces, rows), 1) // 8)
    all_k = mm(halo_t.astype(F32).astype(BF), spread)
    wanted = offset + (iota((count, rows), 1) % 8) % block
    keep = wanted == iota((count, rows), 0)
    return jnp.sum(jnp.where(keep, all_k, 0.0), axis=0, keepdims=True).astype(jnp.int32)


def silu_parts(v):
    s = 1.0 / (1.0 + jnp.exp(-v))
    return v * s, s * (1.0 + v * (1.0 - s))


def pack_kernel(region_ref, node_ref, halo_ref, mesh_ref, w_ref, grid_ref, out_ref):
    rows, width = grid_ref.shape
    half = width // 2
    spaces = halo_ref.shape[2]
    slots = spaces * 8
    region = region_ref[...]
    member = one_hot(iota((spaces, rows), 0), region)
    before = (iota((rows, rows), 0) < iota((rows, rows), 1)).astype(F32).astype(BF)
    earlier = mm(member, before)
    rank = jnp.sum(earlier * member.astype(F32), axis=0, keepdims=True).astype(jnp.int32)
    place = iota((slots, rows), 0) == region * 8 + rank
    label = (node_ref[...] + 1).astype(F32)
    labels = jnp.sum(jnp.where(place, label, 0.0), axis=1, keepdims=True)
    wide = out_ref.shape[1]
    out_ref.put(jnp.broadcast_to(labels, (slots, 128)).astype(BF), 2 * width + half, wide)
    halo_t = halo_ref[...].reshape(halo_ref.shape[0], spaces)
    first = halo_column(halo_t, 8, 0)
    rest = halo_column(halo_t, 4, 8)
    mesh = mesh_ref[...]
    ids = iota((slots, mesh.shape[0]), 1)
    out_ref.put(mm(one_hot(first, ids), mesh).astype(BF), 0, width)
    tail = mm(one_hot(rest, ids), mesh)
    left = iota((slots, half), 0) % 8 < 4
    tail = jnp.where(left, tail[:, :half], tail[:, half:]).astype(BF)
    out_ref.put(tail, width, width + half)
    message = silu_parts(mm(grid_ref[...], w_ref[...]))[0].astype(BF)
    placed = mm(place.astype(F32).astype(BF), message).astype(BF)
    out_ref.put(placed, width + half, 2 * width + half)


def table_ids(shape, dim, nodes, count):
    index = iota(shape, dim)
    j = index % 8
    base = nodes + index // 8 * count
    tail = base + 8 + j % 4
    return base + j, jnp.where(j < 4, tail, -1), jnp.where(j < 4, -1, tail)


def ready_kernel(
    sender_ref,
    receiver_ref,
    mesh_ref,
    halo_ref,
    edge_ref,
    w_in_ref,
    base_ref,
    local_ref,
    pick_whole_ref,
    pick_left_ref,
    pick_right_ref,
    pick_receiver_ref,
    sum_receiver_ref,
    sum_sender_ref,
    send_whole_ref,
    send_tail_ref,
    back_whole_ref,
    back_left_ref,
    back_right_ref,
    count,
):
    edges, width = edge_ref.shape
    nodes = mesh_ref.shape[0]
    slots = pick_whole_ref.shape[1]
    sender_row, receiver_row = sender_ref[...], receiver_ref[...]
    sender, receiver = column_of(sender_row), column_of(receiver_row)
    ids = iota((edges, nodes), 1)
    pick_receiver = one_hot(receiver, ids)
    pick_receiver_ref.put(pick_receiver)
    mesh = mesh_ref[...]
    receiver_rows = mm(pick_receiver, mesh).astype(BF)
    local_ref.put(mm(one_hot(sender, ids), mesh).astype(BF))
    base = mm(edge_ref[...], w_in_ref[:width, :])
    base_ref.put(base + mm(receiver_rows, w_in_ref[2 * width :, :]))
    whole, left, right = table_ids((1, slots), 1, nodes, count)
    pick_whole_ref.put(one_hot(sender, whole))
    pick_left_ref.put(one_hot(sender, left))
    pick_right_ref.put(one_hot(sender, right))
    ids = iota((nodes, edges), 0)
    sum_receiver_ref.put(one_hot(ids, receiver_row))
    sum_sender_ref.put(one_hot(ids, sender_row))
    whole, left, right = table_ids((slots, 1), 0, nodes, count)
    send_whole_ref.put(one_hot(whole, sender_row))
    send_tail_ref.put(one_hot(jnp.maximum(left, right), sender_row))
    halo_t = halo_ref[...].reshape(count, slots // 8)
    ids = iota((nodes, slots), 0)
    back_whole_ref.put(one_hot(ids, halo_row(halo_t, 8, 0)))
    rest = halo_row(halo_t, 4, 8)
    is_left = iota((1, slots), 1) % 8 < 4
    back_left_ref.put(one_hot(ids, jnp.where(is_left, rest, -1)))
    back_right_ref.put(one_hot(ids, jnp.where(is_left, -1, rest)))


def edge_forward_kernel(
    got_ref,
    pick_whole_ref,
    pick_left_ref,
    pick_right_ref,
    local_ref,
    w_mid_ref,
    base_ref,
    w_out_ref,
    edge_ref,
    sum_receiver_ref,
    node_in_ref,
    node_out_ref,
    mesh_ref,
    cot_ref,
    pick_receiver_ref,
    sums_ref,
    new_ref,
    slope_ref,
    xhat_ref,
    rstd_ref,
):
    edges, width = edge_ref.shape
    half = width // 2
    slots = got_ref.shape[0]
    feats, share, _ = sums_ref.shape
    nodes = feats * share
    label = got_ref[:, 2 * width + half :].astype(F32).T[0:1, :].astype(jnp.int32)
    grid_sum = mm(
        one_hot(iota((nodes, slots), 0) + 1, label), got_ref[:, width + half : 2 * width + half]
    ).astype(BF)
    sums_ref.put(grid_sum.reshape(feats, share, width), width, 2 * width)
    head = mm(pick_whole_ref[...], got_ref[:, :width])
    tail = got_ref[:, width : width + half]
    tails = [mm(pick_left_ref[...], tail), mm(pick_right_ref[...], tail)]
    head = head + jnp.concatenate(tails, 1) + local_ref[...].astype(F32)
    v = mm(head.astype(BF), w_mid_ref[...]) + base_ref[...]
    act, slope = silu_parts(v)
    slope_ref[...] = slope
    u = mm(act.astype(BF), w_out_ref[...])
    center = u - jnp.mean(u, -1, keepdims=True)
    rstd = lax.rsqrt(jnp.mean(center * center, -1, keepdims=True) + 1e-05)
    xhat = center * rstd
    xhat_ref[...] = xhat
    rstd_ref[...] = jnp.broadcast_to(rstd, rstd_ref.shape)
    new = (edge_ref[...].astype(F32) + xhat).astype(BF)
    new_ref.put(new)
    edge_sum = mm(sum_receiver_ref[...], new).astype(BF)
    sums_ref.put(edge_sum.reshape(feats, share, width), 0, width)


def node_kernel(
    sums_ref,
    mesh_ref,
    w_in_ref,
    w_out_ref,
    cot_ref,
    cot_edges_ref,
    send_whole_ref,
    send_tail_ref,
    w_last_ref,
    sum_sender_ref,
    spread_ref,
    new_ref,
    own_ref,
):
    width = mesh_ref.shape[1]
    mesh = mesh_ref[...]
    cot = cot_ref[...].astype(F32)
    sums = jnp.sum(sums_ref[...].astype(F32), axis=0)
    edge_sum = sums[:, :width].astype(BF)
    grid_sum = sums[:, width:].astype(BF)
    v = (
        mm(mesh, w_in_ref[:width, :])
        + mm(grid_sum, w_in_ref[width : 2 * width, :])
        + mm(edge_sum, w_in_ref[2 * width :, :])
    )
    act, slope = silu_parts(v)
    u = mm(act.astype(BF), w_out_ref[...])
    center = u - jnp.mean(u, -1, keepdims=True)
    rstd = lax.rsqrt(jnp.mean(center * center, -1, keepdims=True) + 1e-05)
    xhat = center * rstd
    new_ref[...] = (mesh.astype(F32) + xhat).astype(BF)
    du = norm_back(cot, xhat, rstd)
    dh = mm_nt(du.astype(BF), w_out_ref[...]).astype(BF)
    dv = (dh.astype(F32) * slope).astype(BF)
    sum_grad = mm_nt(dv, w_in_ref[2 * width :, :]).astype(BF)
    spread_ref[...] = jnp.broadcast_to(sum_grad[None], spread_ref.shape)
    own_ref.put(cot + mm_nt(dv, w_in_ref[:width, :]).astype(BF).astype(F32))


def norm_back(cot, xhat, rstd):
    return rstd * (
        cot
        - jnp.mean(cot, -1, keepdims=True)
        - xhat * jnp.mean(cot * xhat, -1, keepdims=True)
    )


def edge_back_kernel(
    grads_ref,
    cot_ref,
    w_out_ref,
    w_mid_ref,
    pick_receiver_ref,
    xhat_ref,
    rstd_ref,
    slope_ref,
    send_whole_ref,
    send_tail_ref,
    w_last_ref,
    sum_sender_ref,
    sum_receiver_ref,
    new_ref,
    send_ref,
    edge_cot_ref,
    dv_ref,
    local_ref,
    new_again_ref,
):
    edges, width = cot_ref.shape
    half = width // 2
    slots = send_ref.shape[0]
    spread = mm(pick_receiver_ref[...], grads_ref[...])
    cot = (cot_ref[...].astype(F32) + spread).astype(BF)
    edge_cot_ref.put(cot)
    new_again_ref.put(new_ref[...])
    du = norm_back(cot.astype(F32), xhat_ref[...], rstd_ref[:, 0:1])
    dh = mm_nt(du.astype(BF), w_out_ref[...]).astype(BF)
    dv = (dh.astype(F32) * slope_ref[...]).astype(BF)
    dv_ref.put(dv)
    sgrad = mm_nt(dv, w_mid_ref[...]).astype(BF)
    send_ref.put(mm(send_whole_ref[...], sgrad).astype(BF), 0, width)
    tail = mm(send_tail_ref[...], sgrad)
    left = iota((slots, half), 0) % 8 < 4
    tail = jnp.where(left, tail[:, :half], tail[:, half:]).astype(BF)
    send_ref.put(tail, width, width + half)
    rgrad = mm_nt(dv, w_last_ref[...]).astype(BF)
    local_ref.put(mm(sum_sender_ref[...], sgrad) + mm(sum_receiver_ref[...], rgrad))


def edge_grad_kernel(parts_ref, dv_ref, w_first_ref, edge_cot_ref, grad_ref):
    direct = mm_nt(dv_ref[...], w_first_ref[...]).astype(BF)
    grad_ref.put((edge_cot_ref[...].astype(F32) + direct.astype(F32)).astype(BF))


def return_kernel(
    got_ref, whole_ref, left_ref, right_ref, local_ref, new_ref, out_ref, new_out_ref
):
    new_out_ref.put(new_ref[...])
    width = local_ref.shape[1]
    total = mm(whole_ref[...], got_ref[:, :width])
    tail = got_ref[:, width:]
    total = total + jnp.concatenate([mm(left_ref[...], tail), mm(right_ref[...], tail)], 1)
    total = total + local_ref[...]
    out_ref.put(total.astype(BF).reshape(out_ref.shape))


def finish_kernel(got_ref, own_ref, out_ref):
    out_ref.put((jnp.sum(got_ref[...].astype(F32), axis=0) + own_ref[...]).astype(BF))


def swap(values, axis):
    return lax.all_to_all(values, axis, split_axis=0, concat_axis=0, tiled=True)


def body(
    grid_latents,
    grid_region,
    grid_node,
    mesh_latents,
    edge_latents,
    edge_sender,
    edge_receiver,
    halo_send,
    w_grid,
    w_edge_in,
    w_edge_out,
    w_node_in,
    w_node_out,
    cot_mesh,
    cot_edges,
):
    spaces = lax.axis_size("space")
    feats = lax.axis_size("feat")
    nodes, width = mesh_latents.shape
    edges = edge_latents.shape[0]
    count = halo_send.shape[2]
    share = nodes // feats
    slots = spaces * 8
    back = width + width // 2
    region_row = grid_region.reshape(1, -1)
    node_row = grid_node.reshape(1, -1)
    sender = edge_sender.reshape(1, -1)
    receiver = edge_receiver.reshape(1, -1)
    halo_t = halo_send.transpose(2, 0, 1)
    wide = 2 * width + width // 2 + 128

    def own_start():
        return pl.multiple_of(lax.axis_index("feat") * share, share)

    (packed,) = call(
        pack_kernel,
        [Push((slots, wide), BF)],
        [
            Fetch(array)
            for array in (region_row, node_row, halo_t, mesh_latents, w_grid, grid_latents)
        ],
    )
    got = swap(packed.reshape(spaces, 8, wide), "space").reshape(slots, wide)
    (
        base,
        sender_local,
        pick_whole,
        pick_left,
        pick_right,
        pick_receiver,
        sum_receiver,
        sum_sender,
        send_whole,
        send_tail,
        back_whole,
        back_left,
        back_right,
    ) = call(
        functools.partial(ready_kernel, count=count),
        [Push((edges, width), F32), Push((edges, width), BF)]
        + [Push((edges, slots), BF)] * 3
        + [Push((edges, nodes), BF)]
        + [Push((nodes, edges), BF)] * 2
        + [Push((slots, edges), BF)] * 2
        + [Push((nodes, slots), BF)] * 3,
        [
            Fetch(array)
            for array in (sender, receiver, mesh_latents, halo_t, edge_latents, w_edge_in)
        ],
    )
    (
        sums,
        new_edges,
        slope,
        xhat,
        rstd,
        w_mid,
        w_out,
        sum_receiver,
        node_in,
        node_out,
        mesh_own,
        cot_own,
        pick_receiver,
    ) = call(
        edge_forward_kernel,
        [
            Push((feats, share, 2 * width), BF),
            Push((edges, width), BF),
            ((edges, width), F32),
            ((edges, width), F32),
            ((edges, 128), F32),
        ],
        [
            got,
            Fetch(pick_whole),
            Fetch(pick_left),
            Fetch(pick_right),
            Fetch(sender_local),
            Fetch(w_edge_in, rows=width, start=width, keep=True),
            Fetch(base),
            Fetch(w_edge_out, keep=True),
            Fetch(edge_latents),
            Fetch(sum_receiver, keep=True),
            Fetch(w_node_in, keep=True),
            Fetch(w_node_out, keep=True),
            Fetch(mesh_latents, rows=share, start=own_start, keep=True),
            Fetch(cot_mesh, rows=share, start=own_start, keep=True),
            Fetch(pick_receiver, keep=True),
        ],
    )
    sums = swap(sums, "feat")
    spread, new_share, own, edge_cot, send_whole, send_tail, w_last, sum_sender = call(
        node_kernel,
        [((feats, share, width), BF), ((share, width), BF), Push((share, width), F32)],
        [
            sums,
            mesh_own,
            node_in,
            node_out,
            cot_own,
            Fetch(cot_edges, keep=True),
            Fetch(send_whole, keep=True),
            Fetch(send_tail, keep=True),
            Fetch(w_edge_in, rows=width, start=2 * width, keep=True),
            Fetch(sum_sender, keep=True),
        ],
    )
    grads = swap(spread, "feat").reshape(nodes, width)
    send, edge_cot, dv, local, new_share = call(
        edge_back_kernel,
        [
            Push((slots, back), BF),
            Push((edges, width), BF),
            Push((edges, width), BF),
            Push((nodes, width), F32),
            Push((share, width), BF),
        ],
        [
            grads,
            edge_cot,
            w_out,
            w_mid,
            pick_receiver,
            xhat,
            rstd,
            slope,
            send_whole,
            send_tail,
            w_last,
            sum_sender,
            sum_receiver,
            new_share,
        ],
    )
    returned = swap(send.reshape(spaces, 8, back), "space").reshape(slots, back)
    new_mesh = lax.all_gather(new_share, "feat", axis=0, tiled=True)
    parts, new_mesh = call(
        return_kernel,
        [Push((feats, share, width), BF), Push((nodes, width), BF)],
        [
            returned,
            Fetch(back_whole),
            Fetch(back_left),
            Fetch(back_right),
            Fetch(local),
            new_mesh,
        ],
    )
    last = swap(parts, "feat")
    (grad_edges,) = call(
        edge_grad_kernel,
        [Push((edges, width), BF)],
        [
            Fetch(parts, rows=1, start=0),
            Fetch(dv),
            Fetch(w_edge_in, rows=width, start=0),
            Fetch(edge_cot),
        ],
    )
    (grad_mesh,) = call(finish_kernel, [Push((share, width), BF)], [last, Fetch(own)])
    return new_mesh, new_edges, grad_mesh, grad_edges


def solution(mesh):
    return jax.shard_map(
        body,
        mesh=mesh,
        in_specs=(
            P(("space", "feat"), None),
            P(("space", "feat"), None),
            P(("space", "feat")),
            P("space", None),
            P(("space", "feat"), None),
            P(("space", "feat")),
            P(("space", "feat")),
            P("space", None, None),
            P(),
            P(),
            P(),
            P(),
            P(),
            P("space", None),
            P(("space", "feat"), None),
        ),
        out_specs=(
            P("space", None),
            P(("space", "feat"), None),
            P(("space", "feat"), None),
            P(("space", "feat"), None),
        ),
        check_vma=False,
    )
```

time: 174 us -> 167 us (0.960)
  blocking collectives: 57.8 us -> 72.7 us
  waiting for transfers between devices: 54.1 us -> 42.2 us
  local copies, waits for them, and re-layouts: 12.4 us -> 1.15 us
  Pallas kernels: 15.2 us -> 24.2 us
  starting transfers between devices: 33.1 us -> 24.8 us
    all_to_all x2, blocking collectives: 35.5 us -> 50.5 us  [swap(): return lax.all_to_all(values, axis, split_axis=0, concat_axis=0, tiled=True)]
    unnamed x53 -> x6, local copies, waits for them, and re-layouts: 12.4 us -> 0.02 us
    all_to_all x3, waiting for transfers between devices: 54.1 us -> 42.2 us  [swap(): return lax.all_to_all(values, axis, split_axis=0, concat_axis=0, tiled=True)]
    pallas_call x7 -> x8, Pallas kernels: 15.2 us -> 24.2 us  [call(): pl.pallas_call(run, out_shape=out_shape + [pltpu.VMEM(arg.shape, arg.arra...]
    all_to_all x3, starting transfers between devices: 33.1 us -> 24.8 us  [swap(): return lax.all_to_all(values, axis, split_axis=0, concat_axis=0, tiled=True)]
  transfers between devices with their start and end apart: 3 -> 3, of which waited for: 2 -> 2; matrix products, arithmetic and copies ran while one was open for 0% -> 1% of each run, Pallas kernels for 1% -> 4%
where the time goes in v2:
time: 167 us; the launch traced here: 166 us
  blocking collectives  72.7 us (44%)
  waiting for transfers between devices  42.2 us (25%)
  starting transfers between devices  24.8 us (15%)
  Pallas kernels  24.2 us (14%)
    all_to_all x2, blocking collectives, swap(): return lax.all_to_all(values, axis, split_axis=0, concat_axis=0, tiled=True)  50.5 us
    all_to_all x3, waiting for transfers between devices, swap(): return lax.all_to_all(values, axis, split_axis=0, concat_axis=0, tiled=True)  42.2 us
    all_to_all x3, starting transfers between devices, swap(): return lax.all_to_all(values, axis, split_axis=0, concat_axis=0, tiled=True)  24.8 us
    pallas_call x8, Pallas kernels, call(): pl.pallas_call(run, out_shape=out_shape + [pltpu.VMEM(arg.shape, arg.arra...  24.2 us
    all_gather x1, blocking collectives, body(): new_mesh = lax.all_gather(new_share, 'feat', axis=0, tiled=True)  22.2 us
  transfers between devices with their start and end apart: 3, of which 2 were waited for; matrix products, arithmetic and copies ran while one was open for 1% of the time, Pallas kernels for 4%

profile of v2, /device:TPU:6, one launch (start us, length us, event | category | flops | bytes accessed | tf_op | source)
XLA Modules:
  0.0 165.8 jit_solution(14984753793345164909)
XLA Ops:
  0.6 3.4 %shard_map.174 = bf16[512,1408]{1,0:T(8,128)(2,1)} custom-call(s32[1,256]{1,0:T(1,128)} %bitcast.15, s32[1,256]{1,0:T(1,128)} %bitcast.16, s32[12,1,64]{2,1,0:T(1,128)} %bitcast.13, bf16[192,512]{1,0:T(8,128)(2,1)} %refs_12_.1, bf16[512,512]{1,0:T(8,128)(2,1)} %refs_4_.2, bf16[256,512]{1,0:T(8,128)(2,1)} %refs_5_.4), custom_call_target="tpu_custom_call" | custom-call | tf_op jit(solution)/shard_map/pallas_call | solution.py:126
  4.1 0.0 copy-start.1
  4.1 0.0 copy-start.2
  4.1 13.9 %all-to-all-start = ((bf16[64,8,1408]{2,1,0:T(8,128)(2,1)}), bf16[64,8,1408]{2,1,0:T(8,128)(2,1)S(1)}, u32[]{:S(2)}, u32[]{:S(2)}) async-start(bf16[64,8,1408]{2,1,0:T(8,128)(2,1)} %bitcast.11), calls=%async_computation | async-start | bytes 2883584 | tf_op jit(solution)/shard_map/all_to_all | solution.py:424
  18.0 0.0 copy-done.1
  18.1 0.6 reshape.39.refs_0_
  18.6 0.0 copy-done.2
  18.6 0.6 reshape.40.refs_1_
  19.2 4.6 %shard_map.175 = (f32[384,512]{1,0:T(8,128)}, bf16[384,512]{1,0:T(8,128)(2,1)}, bf16[384,512]{1,0:T(8,128)(2,1)}, bf16[384,512]{1,0:T(8,128)(2,1)}, bf16[384,512...) custom-call(s32[1,384]{1,0:T(1,128)} %reshape.39.refs_0_, ...), custom_call_target="tpu_custom_call" | custom-call | tf_op jit(solution)/shard_map/pallas_call | solution.py:126
  23.8 29.1 %all-to-all-done = bf16[64,8,1408]{2,1,0:T(8,128)(2,1)S(1)} async-done(((bf16[64,8,1408]{2,1,0:T(8,128)(2,1)}), bf16[64,8,1408]{2,1,0:T(8,128)(2,1)S(1)}, u32[]{:S(2)}, u32[]{:S(2)}) %all-to-all-start) | async-done | bytes 1441824 | tf_op jit(solution)/shard_map/all_to_all | solution.py:424
  52.9 4.5 %shard_map.176 = (bf16[12,16,1024]{2,1,0:T(8,128)(2,1)}, bf16[384,512]{1,0:T(8,128)(2,1)}, f32[384,512]{1,0:T(8,128)S(1)}, f32[384,512]{1,0:T(8,128)S(1)}, f32[3...) custom-call(bf16[512,1408]{1,0:T(8,128)(2,1)S(1)} %bitcast.8, ...), custom_call_target="tpu_custom_call" | custom-call | tf_op jit(solution)/shard_map/pallas_call | solution.py:126
  57.4 31.3 %all_to_all.25.refs_0_ = bf16[12,16,1024]{2,1,0:T(8,128)(2,1)S(1)} all-to-all(bf16[12,16,1024]{2,1,0:T(8,128)(2,1)} %get-tuple-element.52), channel_id=1, replica_groups=mesh['space'=64,'feat'=12] {'feat'}, dimensions={0} | all-to-all | bytes 786432 | tf_op jit(solution)/shard_map/all_to_all | solution.py:424
  88.8 2.2 %shard_map.177 = (bf16[12,16,512]{2,1,0:T(8,128)(2,1)S(1)}, bf16[16,512]{1,0:T(8,128)(2,1)S(1)}, f32[16,512]{1,0:T(8,128)}, bf16[384,512]{1,0:T(8,128)(2,1)S(1)}...) custom-call(bf16[12,16,1024]{2,1,0:T(8,128)(2,1)S(1)} %all_to_all.25, ...), custom_call_target="tpu_custom_call" | custom-call | tf_op jit(solution)/shard_map/pallas_call | solution.py:126
  90.9 19.2 %all_to_all.26 = bf16[12,16,512]{2,1,0:T(8,128)(2,1)S(1)} all-to-all(bf16[12,16,512]{2,1,0:T(8,128)(2,1)S(1)} %get-tuple-element.60), channel_id=1, replica_groups=mesh['space'=64,'feat'=12] {'feat'}, dimensions={0} | all-to-all | bytes 393216 | tf_op jit(solution)/shard_map/all_to_all | solution.py:424
  110.1 3.1 %shard_map.178 = (bf16[512,768]{1,0:T(8,128)(2,1)}, bf16[384,512]{1,0:T(8,128)(2,1)}, bf16[384,512]{1,0:T(8,128)(2,1)}, f32[192,512]{1,0:T(8,128)}, bf16[16,512]{1,0:T(8,128)(2,1)}) custom-call(bf16[192,512]{1,0:T(8,128)(2,1)S(1)} %bitcast.10, bf16[384,512]{1,0:T(8,128)(2,1)S(1)} %get-tuple-element.61.refs_1_, ...), custom_call_target="tpu_custom_call" | custom-call | tf_op jit(solution)/shard_map/pallas_call | solution.py:126
  113.3 0.0 copy-start
  113.3 6.9 %all-to-all-start.3 = ((bf16[64,8,768]{2,1,0:T(8,128)(2,1)}), bf16[64,8,768]{2,1,0:T(8,128)(2,1)S(1)}, u32[]{:S(2)}, u32[]{:S(2)}) async-start(bf16[64,8,768]{2,1,0:T(8,128)(2,1)} %bitcast.12), calls=%async_computation.3 | async-start | bytes 1572864 | tf_op jit(solution)/shard_map/all_to_all | solution.py:424
  120.2 0.0 copy-done
  120.2 22.2 %all_gather.3.refs_5_ = bf16[192,512]{1,0:T(8,128)(2,1)S(1)} all-gather(bf16[16,512]{1,0:T(8,128)(2,1)S(1)} %copy-done), channel_id=1, replica_groups=mesh['space'=64,'feat'=12] {'feat'}, dimensions={0}, use_global_device_ids=true | all-gather | bytes 212992 | tf_op jit(solution)/shard_map/all_gather | solution.py:584
  142.4 0.0 all-to-all-done.3
  142.4 2.4 %shard_map.179 = (bf16[12,16,512]{2,1,0:T(8,128)(2,1)}, bf16[192,512]{1,0:T(8,128)(2,1)}) custom-call(bf16[512,768]{1,0:T(8,128)(2,1)S(1)} %bitcast.9, bf16[192,512]{1,0:T(8,128)(2,1)} %get-tuple-element.75.refs_1_, bf16[192,512]{1,0:T(8,128)(2,1)} %get-tuple-element.76.refs_2_, bf16[192,512]{1,0:T(8,128)(2,1)} %get-tuple-element.77.refs_3_, ...), custom_call_target="tpu_custom_call" | custom-call | tf_op jit(solution)/shard_map/pallas_call | solution.py:126
  144.9 4.0 %all-to-all-start.4 = ((bf16[12,16,512]{2,1,0:T(8,128)(2,1)}), bf16[12,16,512]{2,1,0:T(8,128)(2,1)S(1)}, u32[]{:S(2)}, u32[]{:S(2)}) async-start(bf16[12,16,512]{2,1,0:T(8,128)(2,1)} %get-tuple-element.82.refs_0_), calls=%async_computation.4 | async-start | bytes 393216 | tf_op jit(solution)/shard_map/all_to_all | solution.py:424
  148.9 2.5 %shard_map.181 = bf16[384,512]{1,0:T(8,128)(2,1)} custom-call(bf16[12,16,512]{2,1,0:T(8,128)(2,1)} %get-tuple-element.82.refs_0_, bf16[384,512]{1,0:T(8,128)(2,1)} %get-tuple-element.84.refs_1_, bf16[1536,512]{1,0:T(8,128)(2,1)} %refs_2_.3, bf16[384,512]{1,0:T(8,128)(2,1)} %get-tuple-element.85.refs_3_), custom_call_target="tpu_custom_call" | custom-call | tf_op jit(solution)/shard_map/pallas_call | solution.py:126
  151.4 13.1 %all-to-all-done.4.refs_0_ = bf16[12,16,512]{2,1,0:T(8,128)(2,1)S(1)} async-done(((bf16[12,16,512]{2,1,0:T(8,128)(2,1)}), bf16[12,16,512]{2,1,0:T(8,128)(2,1)S(1)}, u32[]{:S(2)}, u32[]{:S(2)}) %all-to-all-start.4) | async-done | bytes 196640 | tf_op jit(solution)/shard_map/all_to_all | solution.py:424
  164.4 1.4 shard_map.180
Async XLA Ops:
  4.1 14.0 %copy-start.1 = (s32[384]{0:T(512)S(1)}, s32[384]{0:T(512)}, u32[]{:S(2)}) copy-start(s32[384]{0:T(512)} %param.20) | copy-start | bytes 4612
  4.1 14.5 %copy-start.2 = (s32[384]{0:T(512)S(1)}, s32[384]{0:T(512)}, u32[]{:S(2)}) copy-start(s32[384]{0:T(512)} %param.21) | copy-start | bytes 4612
  4.1 48.8 %all-to-all-start = ((bf16[64,8,1408]{2,1,0:T(8,128)(2,1)}), bf16[64,8,1408]{2,1,0:T(8,128)(2,1)S(1)}, u32[]{:S(2)}, u32[]{:S(2)}) async-start(bf16[64,8,1408]{2,1,0:T(8,128)(2,1)} %bitcast.11), calls=%async_computation | async-start | bytes 2883584 | tf_op jit(solution)/shard_map/all_to_all | solution.py:424
  113.3 6.9 %copy-start = (bf16[16,512]{1,0:T(8,128)(2,1)S(1)}, bf16[16,512]{1,0:T(8,128)(2,1)}, u32[]{:S(2)}) copy-start(bf16[16,512]{1,0:T(8,128)(2,1)} %get-tuple-element.79) | copy-start | bytes 49156
  113.3 29.1 %all-to-all-start.3 = ((bf16[64,8,768]{2,1,0:T(8,128)(2,1)}), bf16[64,8,768]{2,1,0:T(8,128)(2,1)S(1)}, u32[]{:S(2)}, u32[]{:S(2)}) async-start(bf16[64,8,768]{2,1,0:T(8,128)(2,1)} %bitcast.12), calls=%async_computation.3 | async-start | bytes 1572864 | tf_op jit(solution)/shard_map/all_to_all | solution.py:424
  144.9 19.6 %all-to-all-start.4 = ((bf16[12,16,512]{2,1,0:T(8,128)(2,1)}), bf16[12,16,512]{2,1,0:T(8,128)(2,1)S(1)}, u32[]{:S(2)}, u32[]{:S(2)}) async-start(bf16[12,16,512]{2,1,0:T(8,128)(2,1)} %get-tuple-element.82.refs_0_), calls=%async_computation.4 | async-start | bytes 393216 | tf_op jit(solution)/shard_map/all_to_all | solution.py:424

commit v3 on v2

--- a/solution.py
+++ b/solution.py
@@ -35,8 +35,8 @@
 
 
 class Fetch:
-    def __init__(self, array, rows=None, start=None, keep=False):
-        self.array, self.start, self.keep = array, start, keep
+    def __init__(self, array, rows=None, start=None, keep=False, defer=False):
+        self.array, self.start, self.keep, self.defer = array, start, keep, defer
         self.shape = array.shape if rows is None else (rows,) + array.shape[1:]
 
     def source(self, ref):
@@ -51,12 +51,20 @@
 
 
 class Late:
-    def __init__(self, source, target, sem):
-        self.ref, self.shape, self.waited = target, target.shape, False
+    def __init__(self, source, target, sem, defer):
+        self.ref, self.shape = target, target.shape
+        self.started = self.waited = False
         self.copy = pltpu.make_async_copy(source, target, sem)
-        self.copy.start()
+        if not defer:
+            self.start()
+
+    def start(self):
+        if not self.started:
+            self.copy.start()
+            self.started = True
 
     def wait(self):
+        self.start()
         if not self.waited:
             self.copy.wait()
             self.waited = True
@@ -83,6 +91,14 @@
         copy.start()
         self.copies.append(copy)
 
+    def __setitem__(self, index, value):
+        self.ref[index] = value
+
+    def finish(self):
+        if not self.copies:
+            self.copies.append(pltpu.make_async_copy(self.ref, self.target, next(self.sems)))
+            self.copies[0].start()
+
     def wait(self):
         for copy in self.copies:
             copy.wait()
@@ -104,11 +120,14 @@
         for arg, ref in zip(args, ins):
             if isinstance(arg, Fetch):
                 target = next(kept_refs if arg.keep else scratch)
-                ref = Late(arg.source(ref), target, next(sems))
+                ref = Late(arg.source(ref), target, next(sems), arg.defer)
             given.append(ref)
         for out, ref in zip(outs, plain_outs):
             given.append(Out(ref, next(scratch), sems) if isinstance(out, Push) else ref)
         kernel(*given)
+        for ref in given:
+            if isinstance(ref, Out):
+                ref.finish()
         for ref in given:
             if isinstance(ref, (Late, Out)):
                 ref.wait()
@@ -204,81 +223,37 @@
     return base + j, jnp.where(j < 4, tail, -1), jnp.where(j < 4, -1, tail)
 
 
-def ready_kernel(
+def ready_kernel(sender_ref, receiver_ref, mesh_ref, edge_ref, w_in_ref, base_ref, local_ref):
+    edges, width = edge_ref.shape
+    nodes = mesh_ref.shape[0]
+    ids = iota((edges, nodes), 1)
+    mesh = mesh_ref[...]
+    receiver_rows = mm(one_hot(column_of(receiver_ref[...]), ids), mesh).astype(BF)
+    local_ref.put(mm(one_hot(column_of(sender_ref[...]), ids), mesh).astype(BF))
+    base = mm(edge_ref[...], w_in_ref[:width, :])
+    base_ref.put(base + mm(receiver_rows, w_in_ref[2 * width :, :]))
+
+
+def edge_forward_kernel(
+    got_ref,
     sender_ref,
     receiver_ref,
-    mesh_ref,
-    halo_ref,
-    edge_ref,
-    w_in_ref,
-    base_ref,
-    local_ref,
-    pick_whole_ref,
-    pick_left_ref,
-    pick_right_ref,
-    pick_receiver_ref,
-    sum_receiver_ref,
-    sum_sender_ref,
-    send_whole_ref,
-    send_tail_ref,
-    back_whole_ref,
-    back_left_ref,
-    back_right_ref,
-    count,
-):
-    edges, width = edge_ref.shape
-    nodes = mesh_ref.shape[0]
-    slots = pick_whole_ref.shape[1]
-    sender_row, receiver_row = sender_ref[...], receiver_ref[...]
-    sender, receiver = column_of(sender_row), column_of(receiver_row)
-    ids = iota((edges, nodes), 1)
-    pick_receiver = one_hot(receiver, ids)
-    pick_receiver_ref.put(pick_receiver)
-    mesh = mesh_ref[...]
-    receiver_rows = mm(pick_receiver, mesh).astype(BF)
-    local_ref.put(mm(one_hot(sender, ids), mesh).astype(BF))
-    base = mm(edge_ref[...], w_in_ref[:width, :])
-    base_ref.put(base + mm(receiver_rows, w_in_ref[2 * width :, :]))
-    whole, left, right = table_ids((1, slots), 1, nodes, count)
-    pick_whole_ref.put(one_hot(sender, whole))
-    pick_left_ref.put(one_hot(sender, left))
-    pick_right_ref.put(one_hot(sender, right))
-    ids = iota((nodes, edges), 0)
-    sum_receiver_ref.put(one_hot(ids, receiver_row))
-    sum_sender_ref.put(one_hot(ids, sender_row))
-    whole, left, right = table_ids((slots, 1), 0, nodes, count)
-    send_whole_ref.put(one_hot(whole, sender_row))
-    send_tail_ref.put(one_hot(jnp.maximum(left, right), sender_row))
-    halo_t = halo_ref[...].reshape(count, slots // 8)
-    ids = iota((nodes, slots), 0)
-    back_whole_ref.put(one_hot(ids, halo_row(halo_t, 8, 0)))
-    rest = halo_row(halo_t, 4, 8)
-    is_left = iota((1, slots), 1) % 8 < 4
-    back_left_ref.put(one_hot(ids, jnp.where(is_left, rest, -1)))
-    back_right_ref.put(one_hot(ids, jnp.where(is_left, -1, rest)))
-
-
-def edge_forward_kernel(
-    got_ref,
-    pick_whole_ref,
-    pick_left_ref,
-    pick_right_ref,
     local_ref,
     w_mid_ref,
     base_ref,
     w_out_ref,
     edge_ref,
-    sum_receiver_ref,
+    mesh_ref,
+    cot_ref,
     node_in_ref,
     node_out_ref,
-    mesh_ref,
-    cot_ref,
-    pick_receiver_ref,
+    cot_edges_ref,
     sums_ref,
     new_ref,
     slope_ref,
     xhat_ref,
     rstd_ref,
+    count,
 ):
     edges, width = edge_ref.shape
     half = width // 2
@@ -289,10 +264,14 @@
     grid_sum = mm(
         one_hot(iota((nodes, slots), 0) + 1, label), got_ref[:, width + half : 2 * width + half]
     ).astype(BF)
-    sums_ref.put(grid_sum.reshape(feats, share, width), width, 2 * width)
-    head = mm(pick_whole_ref[...], got_ref[:, :width])
+    sums_ref[:, :, width:] = grid_sum.reshape(feats, share, width)
+    sender = column_of(sender_ref[...])
+    whole, left, right = table_ids((1, slots), 1, nodes, count)
+    head = mm(one_hot(sender, whole), got_ref[:, :width])
     tail = got_ref[:, width : width + half]
-    tails = [mm(pick_left_ref[...], tail), mm(pick_right_ref[...], tail)]
+    tails = [mm(one_hot(sender, left), tail), mm(one_hot(sender, right), tail)]
+    for later in (mesh_ref, cot_ref, node_in_ref, node_out_ref, cot_edges_ref):
+        later.start()
     head = head + jnp.concatenate(tails, 1) + local_ref[...].astype(F32)
     v = mm(head.astype(BF), w_mid_ref[...]) + base_ref[...]
     act, slope = silu_parts(v)
@@ -305,8 +284,9 @@
     rstd_ref[...] = jnp.broadcast_to(rstd, rstd_ref.shape)
     new = (edge_ref[...].astype(F32) + xhat).astype(BF)
     new_ref.put(new)
-    edge_sum = mm(sum_receiver_ref[...], new).astype(BF)
-    sums_ref.put(edge_sum.reshape(feats, share, width), 0, width)
+    to_receiver = one_hot(iota((nodes, edges), 0), receiver_ref[...])
+    edge_sum = mm(to_receiver, new).astype(BF)
+    sums_ref[:, :, :width] = edge_sum.reshape(feats, share, width)
 
 
 def node_kernel(
@@ -315,11 +295,8 @@
     w_in_ref,
     w_out_ref,
     cot_ref,
-    cot_edges_ref,
-    send_whole_ref,
-    send_tail_ref,
+    w_first_ref,
     w_last_ref,
-    sum_sender_ref,
     spread_ref,
     new_ref,
     own_ref,
@@ -362,58 +339,58 @@
     cot_ref,
     w_out_ref,
     w_mid_ref,
-    pick_receiver_ref,
+    sender_ref,
+    receiver_ref,
     xhat_ref,
     rstd_ref,
     slope_ref,
-    send_whole_ref,
-    send_tail_ref,
+    w_first_ref,
     w_last_ref,
-    sum_sender_ref,
-    sum_receiver_ref,
     new_ref,
     send_ref,
-    edge_cot_ref,
-    dv_ref,
+    grad_ref,
     local_ref,
     new_again_ref,
+    count,
 ):
+    new_again_ref.put(new_ref[...])
     edges, width = cot_ref.shape
     half = width // 2
+    nodes = grads_ref.shape[0]
     slots = send_ref.shape[0]
-    spread = mm(pick_receiver_ref[...], grads_ref[...])
+    sender, receiver = sender_ref[...], receiver_ref[...]
+    spread = mm(one_hot(column_of(receiver), iota((edges, nodes), 1)), grads_ref[...])
     cot = (cot_ref[...].astype(F32) + spread).astype(BF)
-    edge_cot_ref.put(cot)
-    new_again_ref.put(new_ref[...])
     du = norm_back(cot.astype(F32), xhat_ref[...], rstd_ref[:, 0:1])
     dh = mm_nt(du.astype(BF), w_out_ref[...]).astype(BF)
     dv = (dh.astype(F32) * slope_ref[...]).astype(BF)
-    dv_ref.put(dv)
     sgrad = mm_nt(dv, w_mid_ref[...]).astype(BF)
-    send_ref.put(mm(send_whole_ref[...], sgrad).astype(BF), 0, width)
-    tail = mm(send_tail_ref[...], sgrad)
-    left = iota((slots, half), 0) % 8 < 4
-    tail = jnp.where(left, tail[:, :half], tail[:, half:]).astype(BF)
+    whole, left, right = table_ids((slots, 1), 0, nodes, count)
+    send_ref.put(mm(one_hot(whole, sender), sgrad).astype(BF), 0, width)
+    tail = mm(one_hot(jnp.maximum(left, right), sender), sgrad)
+    tail = jnp.where(left >= 0, tail[:, :half], tail[:, half:]).astype(BF)
     send_ref.put(tail, width, width + half)
     rgrad = mm_nt(dv, w_last_ref[...]).astype(BF)
-    local_ref.put(mm(sum_sender_ref[...], sgrad) + mm(sum_receiver_ref[...], rgrad))
-
-
-def edge_grad_kernel(parts_ref, dv_ref, w_first_ref, edge_cot_ref, grad_ref):
-    direct = mm_nt(dv_ref[...], w_first_ref[...]).astype(BF)
-    grad_ref.put((edge_cot_ref[...].astype(F32) + direct.astype(F32)).astype(BF))
-
-
-def return_kernel(
-    got_ref, whole_ref, left_ref, right_ref, local_ref, new_ref, out_ref, new_out_ref
-):
+    ids = iota((nodes, edges), 0)
+    local_ref.put(mm(one_hot(ids, sender), sgrad) + mm(one_hot(ids, receiver), rgrad))
+    direct = mm_nt(dv, w_first_ref[...]).astype(BF)
+    grad_ref.put((cot.astype(F32) + direct.astype(F32)).astype(BF))
+
+
+def return_kernel(got_ref, halo_ref, local_ref, own_ref, new_ref, out_ref, new_out_ref):
     new_out_ref.put(new_ref[...])
-    width = local_ref.shape[1]
-    total = mm(whole_ref[...], got_ref[:, :width])
+    nodes, width = local_ref.shape
+    slots = got_ref.shape[0]
+    halo_t = halo_ref[...].reshape(halo_ref.shape[0], slots // 8)
+    ids = iota((nodes, slots), 0)
+    total = mm(one_hot(ids, halo_row(halo_t, 8, 0)), got_ref[:, :width])
+    rest = halo_row(halo_t, 4, 8)
+    is_left = iota((1, slots), 1) % 8 < 4
     tail = got_ref[:, width:]
-    total = total + jnp.concatenate([mm(left_ref[...], tail), mm(right_ref[...], tail)], 1)
-    total = total + local_ref[...]
-    out_ref.put(total.astype(BF).reshape(out_ref.shape))
+    left = mm(one_hot(ids, jnp.where(is_left, rest, -1)), tail)
+    right = mm(one_hot(ids, jnp.where(is_left, -1, rest)), tail)
+    total = total + jnp.concatenate([left, right], 1) + local_ref[...]
+    out_ref[...] = total.astype(BF).reshape(out_ref.shape)
 
 
 def finish_kernel(got_ref, own_ref, out_ref):
@@ -468,32 +445,10 @@
         ],
     )
     got = swap(packed.reshape(spaces, 8, wide), "space").reshape(slots, wide)
-    (
-        base,
-        sender_local,
-        pick_whole,
-        pick_left,
-        pick_right,
-        pick_receiver,
-        sum_receiver,
-        sum_sender,
-        send_whole,
-        send_tail,
-        back_whole,
-        back_left,
-        back_right,
-    ) = call(
-        functools.partial(ready_kernel, count=count),
-        [Push((edges, width), F32), Push((edges, width), BF)]
-        + [Push((edges, slots), BF)] * 3
-        + [Push((edges, nodes), BF)]
-        + [Push((nodes, edges), BF)] * 2
-        + [Push((slots, edges), BF)] * 2
-        + [Push((nodes, slots), BF)] * 3,
-        [
-            Fetch(array)
-            for array in (sender, receiver, mesh_latents, halo_t, edge_latents, w_edge_in)
-        ],
+    base, sender_local = call(
+        ready_kernel,
+        [Push((edges, width), F32), Push((edges, width), BF)],
+        [Fetch(array) for array in (sender, receiver, mesh_latents, edge_latents, w_edge_in)],
     )
     (
         sums,
@@ -501,18 +456,19 @@
         slope,
         xhat,
         rstd,
+        sender_held,
+        receiver_held,
         w_mid,
         w_out,
-        sum_receiver,
+        mesh_own,
+        cot_own,
         node_in,
         node_out,
-        mesh_own,
-        cot_own,
-        pick_receiver,
+        edge_cot,
     ) = call(
-        edge_forward_kernel,
-        [
-            Push((feats, share, 2 * width), BF),
+        functools.partial(edge_forward_kernel, count=count),
+        [
+            ((feats, share, 2 * width), BF),
             Push((edges, width), BF),
             ((edges, width), F32),
             ((edges, width), F32),
@@ -520,24 +476,22 @@
         ],
         [
             got,
-            Fetch(pick_whole),
-            Fetch(pick_left),
-            Fetch(pick_right),
+            Fetch(sender, keep=True),
+            Fetch(receiver, keep=True),
             Fetch(sender_local),
             Fetch(w_edge_in, rows=width, start=width, keep=True),
             Fetch(base),
             Fetch(w_edge_out, keep=True),
             Fetch(edge_latents),
-            Fetch(sum_receiver, keep=True),
-            Fetch(w_node_in, keep=True),
-            Fetch(w_node_out, keep=True),
-            Fetch(mesh_latents, rows=share, start=own_start, keep=True),
-            Fetch(cot_mesh, rows=share, start=own_start, keep=True),
-            Fetch(pick_receiver, keep=True),
+            Fetch(mesh_latents, rows=share, start=own_start, keep=True, defer=True),
+            Fetch(cot_mesh, rows=share, start=own_start, keep=True, defer=True),
+            Fetch(w_node_in, keep=True, defer=True),
+            Fetch(w_node_out, keep=True, defer=True),
+            Fetch(cot_edges, keep=True, defer=True),
         ],
     )
     sums = swap(sums, "feat")
-    spread, new_share, own, edge_cot, send_whole, send_tail, w_last, sum_sender = call(
+    spread, new_share, own, w_first, w_last = call(
         node_kernel,
         [((feats, share, width), BF), ((share, width), BF), Push((share, width), F32)],
         [
@@ -546,19 +500,15 @@
             node_in,
             node_out,
             cot_own,
-            Fetch(cot_edges, keep=True),
-            Fetch(send_whole, keep=True),
-            Fetch(send_tail, keep=True),
+            Fetch(w_edge_in, rows=width, start=0, keep=True),
             Fetch(w_edge_in, rows=width, start=2 * width, keep=True),
-            Fetch(sum_sender, keep=True),
         ],
     )
     grads = swap(spread, "feat").reshape(nodes, width)
-    send, edge_cot, dv, local, new_share = call(
-        edge_back_kernel,
+    send, grad_edges, local, new_share = call(
+        functools.partial(edge_back_kernel, count=count),
         [
             Push((slots, back), BF),
-            Push((edges, width), BF),
             Push((edges, width), BF),
             Push((nodes, width), F32),
             Push((share, width), BF),
@@ -568,44 +518,31 @@
             edge_cot,
             w_out,
             w_mid,
-            pick_receiver,
+            sender_held,
+            receiver_held,
             xhat,
             rstd,
             slope,
-            send_whole,
-            send_tail,
+            w_first,
             w_last,
-            sum_sender,
-            sum_receiver,
             new_share,
         ],
     )
     returned = swap(send.reshape(spaces, 8, back), "space").reshape(slots, back)
     new_mesh = lax.all_gather(new_share, "feat", axis=0, tiled=True)
-    parts, new_mesh = call(
+    parts, new_mesh, own = call(
         return_kernel,
-        [Push((feats, share, width), BF), Push((nodes, width), BF)],
+        [((feats, share, width), BF), Push((nodes, width), BF)],
         [
             returned,
-            Fetch(back_whole),
-            Fetch(back_left),
-            Fetch(back_right),
+            Fetch(halo_t),
             Fetch(local),
+            Fetch(own, keep=True),
             new_mesh,
         ],
     )
     last = swap(parts, "feat")
-    (grad_edges,) = call(
-        edge_grad_kernel,
-        [Push((edges, width), BF)],
-        [
-            Fetch(parts, rows=1, start=0),
-            Fetch(dv),
-            Fetch(w_edge_in, rows=width, start=0),
-            Fetch(edge_cot),
-        ],
-    )
-    (grad_mesh,) = call(finish_kernel, [Push((share, width), BF)], [last, Fetch(own)])
+    (grad_mesh,) = call(finish_kernel, [Push((share, width), BF)], [last, own])
     return new_mesh, new_edges, grad_mesh, grad_edges
 
 

time: 167 us -> 162 us (0.970)
  blocking collectives: 72.7 us -> 90.5 us
  waiting for transfers between devices: 42.2 us -> 30.5 us
  Pallas kernels: 24.2 us -> 17.9 us
  starting transfers between devices: 24.8 us -> 20.9 us
    all_to_all x2 -> x3, blocking collectives: 50.5 us -> 68.3 us  [swap(): return lax.all_to_all(values, axis, split_axis=0, concat_axis=0, tiled=True)]
    all_to_all x3 -> x2, waiting for transfers between devices: 42.2 us -> 30.5 us  [swap(): return lax.all_to_all(values, axis, split_axis=0, concat_axis=0, tiled=True)]
    pallas_call x8 -> x7, Pallas kernels: 24.2 us -> 17.9 us  [call(): pl.pallas_call(run, out_shape=out_shape + [pltpu.VMEM(arg.shape, arg.arra...]
    all_to_all x3 -> x2, starting transfers between devices: 24.8 us -> 20.9 us  [swap(): return lax.all_to_all(values, axis, split_axis=0, concat_axis=0, tiled=True)]
  transfers between devices with their start and end apart: 3 -> 2, of which waited for: 2 -> 1; matrix products, arithmetic and copies ran while one was open for 1% -> 1% of each run, Pallas kernels for 4% -> 2%
where the time goes in v3:
time: 162 us
  blocking collectives  90.5 us (56%)
  waiting for transfers between devices  30.5 us (19%)
  starting transfers between devices  20.9 us (13%)
  Pallas kernels  17.9 us (11%)
    all_to_all x3, blocking collectives, swap(): return lax.all_to_all(values, axis, split_axis=0, concat_axis=0, tiled=True)  68.3 us
    all_to_all x2, waiting for transfers between devices, swap(): return lax.all_to_all(values, axis, split_axis=0, concat_axis=0, tiled=True)  30.5 us
    all_gather x1, blocking collectives, body(): new_mesh = lax.all_gather(new_share, 'feat', axis=0, tiled=True)  22.2 us
    all_to_all x2, starting transfers between devices, swap(): return lax.all_to_all(values, axis, split_axis=0, concat_axis=0, tiled=True)  20.9 us
    pallas_call x7, Pallas kernels, call(): pl.pallas_call(run, out_shape=out_shape + [pltpu.VMEM(arg.shape, arg.arra...  17.9 us
  transfers between devices with their start and end apart: 2, of which 1 were waited for; matrix products, arithmetic and copies ran while one was open for 1% of the time, Pallas kernels for 2%

profile of v3, /device:TPU:6, one launch (start us, length us, event | category | flops | bytes accessed | tf_op | source)
XLA Modules:
  0.0 161.6 jit_solution(17213285999295270250)
XLA Ops:
  0.6 3.5 %shard_map.174 = bf16[512,1408]{1,0:T(8,128)(2,1)} custom-call(s32[1,256]{1,0:T(1,128)} %bitcast.15, s32[1,256]{1,0:T(1,128)} %bitcast.16, s32[12,1,64]{2,1,0:T(1,128)} %bitcast.13, bf16[192,512]{1,0:T(8,128)(2,1)} %refs_8_.1, bf16[512,512]{1,0:T(8,128)(2,1)} %refs_4_.3, bf16[256,512]{1,0:T(8,128)(2,1)} %refs_5_.2), custom_call_target="tpu_custom_call" | custom-call | tf_op jit(solution)/shard_map/pallas_call | solution.py:145
  4.1 0.0 copy-start.1
  4.1 0.0 copy-start.2
  4.1 13.9 %all-to-all-start = ((bf16[64,8,1408]{2,1,0:T(8,128)(2,1)}), bf16[64,8,1408]{2,1,0:T(8,128)(2,1)S(1)}, u32[]{:S(2)}, u32[]{:S(2)}) async-start(bf16[64,8,1408]{2,1,0:T(8,128)(2,1)} %bitcast.11), calls=%async_computation | async-start | bytes 2883584 | tf_op jit(solution)/shard_map/all_to_all | solution.py:401
  18.1 0.0 copy-done.1
  18.1 0.6 reshape.39.refs_0_.refs_1_
  18.7 0.0 copy-done.2
  18.7 0.6 reshape.40.refs_1_.refs_2_
  19.2 3.3 %shard_map.175 = (f32[384,512]{1,0:T(8,128)}, bf16[384,512]{1,0:T(8,128)(2,1)}) custom-call(s32[1,384]{1,0:T(1,128)} %reshape.39.refs_0_.refs_1_, s32[1,384]{1,0:T(1,128)} %reshape.40.refs_1_.refs_2_, bf16[192,512]{1,0:T(8,128)(2,1)} %refs_8_.1, bf16[384,512]{1,0:T(8,128)(2,1)} %refs_7_.1, bf16[1536,512]{1,0:T(8,128)(2,1)} %refs_6_.3), custom_call_target="tpu_custom_call" | custom-call | tf_op jit(solution)/shard_map/pallas_call | solution.py:145
  22.5 30.5 %all-to-all-done = bf16[64,8,1408]{2,1,0:T(8,128)(2,1)S(1)} async-done(((bf16[64,8,1408]{2,1,0:T(8,128)(2,1)}), bf16[64,8,1408]{2,1,0:T(8,128)(2,1)S(1)}, u32[]{:S(2)}, u32[]{:S(2)}) %all-to-all-start) | async-done | bytes 1441824 | tf_op jit(solution)/shard_map/all_to_all | solution.py:401
  53.0 3.6 %shard_map.176 = (bf16[12,16,1024]{2,1,0:T(8,128)(2,1)S(1)}, bf16[384,512]{1,0:T(8,128)(2,1)}, f32[384,512]{1,0:T(8,128)S(1)}, f32[384,512]{1,0:T(8,128)S(1)}, f...) custom-call(bf16[512,1408]{1,0:T(8,128)(2,1)S(1)} %bitcast.8, ...), custom_call_target="tpu_custom_call" | custom-call | tf_op jit(solution)/shard_map/pallas_call | solution.py:145
  56.6 31.1 %all_to_all.25.refs_0_ = bf16[12,16,1024]{2,1,0:T(8,128)(2,1)S(1)} all-to-all(bf16[12,16,1024]{2,1,0:T(8,128)(2,1)S(1)} %get-tuple-element.34), channel_id=1, replica_groups=mesh['space'=64,'feat'=12] {'feat'}, dimensions={0} | all-to-all | bytes 786432 | tf_op jit(solution)/shard_map/all_to_all | solution.py:401
  87.7 2.2 %shard_map.177 = (bf16[12,16,512]{2,1,0:T(8,128)(2,1)S(1)}, bf16[16,512]{1,0:T(8,128)(2,1)S(1)}, f32[16,512]{1,0:T(8,128)}, bf16[512,512]{1,0:T(8,128)(2,1)S(1)}, bf16[512,512]{1,0:T(8,128)(2,1)S(1)}) custom-call(bf16[12,16,1024]{2,1,0:T(8,128)(2,1)S(1)} %all_to_all.25.refs_0_, bf16[16,512]{1,0:T(8,128)(2,1)S(1)} %get-tuple-element.35.refs_1_, ...), custom_call_target="tpu_custom_call" | custom-call | tf_op jit(solution)/shard_map/pallas_call | solution.py:145
  90.0 19.2 %all_to_all.26 = bf16[12,16,512]{2,1,0:T(8,128)(2,1)S(1)} all-to-all(bf16[12,16,512]{2,1,0:T(8,128)(2,1)S(1)} %get-tuple-element.39), channel_id=1, replica_groups=mesh['space'=64,'feat'=12] {'feat'}, dimensions={0} | all-to-all | bytes 393216 | tf_op jit(solution)/shard_map/all_to_all | solution.py:401
  109.2 3.4 %shard_map.178 = (bf16[512,768]{1,0:T(8,128)(2,1)}, bf16[384,512]{1,0:T(8,128)(2,1)}, f32[192,512]{1,0:T(8,128)}, bf16[16,512]{1,0:T(8,128)(2,1)}) custom-call(bf16[192,512]{1,0:T(8,128)(2,1)S(1)} %bitcast.10, bf16[384,512]{1,0:T(8,128)(2,1)S(1)} %get-tuple-element.40.refs_1_, bf16[512,512]{1,0:T(8,128)(2,1)S(1)} %get-tuple-element.41.refs_2_, ...), custom_call_target="tpu_custom_call" | custom-call | tf_op jit(solution)/shard_map/pallas_call | solution.py:145
  112.6 0.0 copy-start
  112.6 6.9 %all-to-all-start.3 = ((bf16[64,8,768]{2,1,0:T(8,128)(2,1)}), bf16[64,8,768]{2,1,0:T(8,128)(2,1)S(1)}, u32[]{:S(2)}, u32[]{:S(2)}) async-start(bf16[64,8,768]{2,1,0:T(8,128)(2,1)} %bitcast.12), calls=%async_computation.3 | async-start | bytes 1572864 | tf_op jit(solution)/shard_map/all_to_all | solution.py:401
  119.5 0.0 copy-done
  119.5 22.2 %all_gather.3.refs_4_ = bf16[192,512]{1,0:T(8,128)(2,1)S(1)} all-gather(bf16[16,512]{1,0:T(8,128)(2,1)S(1)} %copy-done), channel_id=1, replica_groups=mesh['space'=64,'feat'=12] {'feat'}, dimensions={0}, use_global_device_ids=true | all-gather | bytes 212992 | tf_op jit(solution)/shard_map/all_gather | solution.py:532
  141.7 0.0 all-to-all-done.3
  141.7 1.3 shard_map.179
  143.0 17.9 %all_to_all.27.refs_0_ = bf16[12,16,512]{2,1,0:T(8,128)(2,1)S(1)} all-to-all(bf16[12,16,512]{2,1,0:T(8,128)(2,1)S(1)} %get-tuple-element.57), channel_id=1, replica_groups=mesh['space'=64,'feat'=12] {'feat'}, dimensions={0} | all-to-all | bytes 393216 | tf_op jit(solution)/shard_map/all_to_all | solution.py:401
  161.0 0.7 shard_map.180
Async XLA Ops:
  4.1 14.0 %copy-start.1 = (s32[384]{0:T(512)S(1)}, s32[384]{0:T(512)}, u32[]{:S(2)}) copy-start(s32[384]{0:T(512)} %param.20) | copy-start | bytes 4612
  4.1 14.5 %copy-start.2 = (s32[384]{0:T(512)S(1)}, s32[384]{0:T(512)}, u32[]{:S(2)}) copy-start(s32[384]{0:T(512)} %param.21) | copy-start | bytes 4612
  4.1 48.8 %all-to-all-start = ((bf16[64,8,1408]{2,1,0:T(8,128)(2,1)}), bf16[64,8,1408]{2,1,0:T(8,128)(2,1)S(1)}, u32[]{:S(2)}, u32[]{:S(2)}) async-start(bf16[64,8,1408]{2,1,0:T(8,128)(2,1)} %bitcast.11), calls=%async_computation | async-start | bytes 2883584 | tf_op jit(solution)/shard_map/all_to_all | solution.py:401
  112.6 6.9 %copy-start = (bf16[16,512]{1,0:T(8,128)(2,1)S(1)}, bf16[16,512]{1,0:T(8,128)(2,1)}, u32[]{:S(2)}) copy-start(bf16[16,512]{1,0:T(8,128)(2,1)} %get-tuple-element.54) | copy-start | bytes 49156
  112.6 29.1 %all-to-all-start.3 = ((bf16[64,8,768]{2,1,0:T(8,128)(2,1)}), bf16[64,8,768]{2,1,0:T(8,128)(2,1)S(1)}, u32[]{:S(2)}, u32[]{:S(2)}) async-start(bf16[64,8,768]{2,1,0:T(8,128)(2,1)} %bitcast.12), calls=%async_computation.3 | async-start | bytes 1572864 | tf_op jit(solution)/shard_map/all_to_all | solution.py:401

commit v4 on v3

--- a/solution.py
+++ b/solution.py
@@ -243,11 +243,15 @@
     base_ref,
     w_out_ref,
     edge_ref,
+    w_grid_sum_ref,
+    w_edge_sum_ref,
     mesh_ref,
     cot_ref,
-    node_in_ref,
+    w_mesh_ref,
     node_out_ref,
     cot_edges_ref,
+    w_first_ref,
+    w_last_ref,
     sums_ref,
     new_ref,
     slope_ref,
@@ -264,14 +268,15 @@
     grid_sum = mm(
         one_hot(iota((nodes, slots), 0) + 1, label), got_ref[:, width + half : 2 * width + half]
     ).astype(BF)
-    sums_ref[:, :, width:] = grid_sum.reshape(feats, share, width)
     sender = column_of(sender_ref[...])
     whole, left, right = table_ids((1, slots), 1, nodes, count)
     head = mm(one_hot(sender, whole), got_ref[:, :width])
     tail = got_ref[:, width : width + half]
     tails = [mm(one_hot(sender, left), tail), mm(one_hot(sender, right), tail)]
-    for later in (mesh_ref, cot_ref, node_in_ref, node_out_ref, cot_edges_ref):
+    for later in (mesh_ref, cot_ref, w_mesh_ref, node_out_ref, cot_edges_ref):
         later.start()
+    w_first_ref.start()
+    w_last_ref.start()
     head = head + jnp.concatenate(tails, 1) + local_ref[...].astype(F32)
     v = mm(head.astype(BF), w_mid_ref[...]) + base_ref[...]
     act, slope = silu_parts(v)
@@ -286,32 +291,24 @@
     new_ref.put(new)
     to_receiver = one_hot(iota((nodes, edges), 0), receiver_ref[...])
     edge_sum = mm(to_receiver, new).astype(BF)
-    sums_ref[:, :, :width] = edge_sum.reshape(feats, share, width)
+    terms = mm(grid_sum, w_grid_sum_ref[...]) + mm(edge_sum, w_edge_sum_ref[...])
+    sums_ref[...] = terms.astype(BF).reshape(feats, share, width)
 
 
 def node_kernel(
     sums_ref,
     mesh_ref,
-    w_in_ref,
+    w_mesh_ref,
+    w_edge_sum_ref,
     w_out_ref,
     cot_ref,
-    w_first_ref,
-    w_last_ref,
     spread_ref,
     new_ref,
     own_ref,
 ):
-    width = mesh_ref.shape[1]
     mesh = mesh_ref[...]
     cot = cot_ref[...].astype(F32)
-    sums = jnp.sum(sums_ref[...].astype(F32), axis=0)
-    edge_sum = sums[:, :width].astype(BF)
-    grid_sum = sums[:, width:].astype(BF)
-    v = (
-        mm(mesh, w_in_ref[:width, :])
-        + mm(grid_sum, w_in_ref[width : 2 * width, :])
-        + mm(edge_sum, w_in_ref[2 * width :, :])
-    )
+    v = mm(mesh, w_mesh_ref[...]) + jnp.sum(sums_ref[...].astype(F32), axis=0)
     act, slope = silu_parts(v)
     u = mm(act.astype(BF), w_out_ref[...])
     center = u - jnp.mean(u, -1, keepdims=True)
@@ -321,9 +318,9 @@
     du = norm_back(cot, xhat, rstd)
     dh = mm_nt(du.astype(BF), w_out_ref[...]).astype(BF)
     dv = (dh.astype(F32) * slope).astype(BF)
-    sum_grad = mm_nt(dv, w_in_ref[2 * width :, :]).astype(BF)
+    sum_grad = mm_nt(dv, w_edge_sum_ref[...]).astype(BF)
     spread_ref[...] = jnp.broadcast_to(sum_grad[None], spread_ref.shape)
-    own_ref.put(cot + mm_nt(dv, w_in_ref[:width, :]).astype(BF).astype(F32))
+    own_ref[...] = cot + mm_nt(dv, w_mesh_ref[...]).astype(BF).astype(F32)
 
 
 def norm_back(cot, xhat, rstd):
@@ -347,13 +344,16 @@
     w_first_ref,
     w_last_ref,
     new_ref,
+    own_ref,
     send_ref,
     grad_ref,
     local_ref,
     new_again_ref,
+    own_again_ref,
     count,
 ):
     new_again_ref.put(new_ref[...])
+    own_again_ref.put(own_ref[...])
     edges, width = cot_ref.shape
     half = width // 2
     nodes = grads_ref.shape[0]
@@ -460,15 +460,18 @@
         receiver_held,
         w_mid,
         w_out,
+        w_edge_sum,
         mesh_own,
         cot_own,
-        node_in,
+        w_mesh,
         node_out,
         edge_cot,
+        w_first,
+        w_last,
     ) = call(
         functools.partial(edge_forward_kernel, count=count),
         [
-            ((feats, share, 2 * width), BF),
+            ((feats, share, width), BF),
             Push((edges, width), BF),
             ((edges, width), F32),
             ((edges, width), F32),
@@ -483,35 +486,32 @@
             Fetch(base),
             Fetch(w_edge_out, keep=True),
             Fetch(edge_latents),
+            Fetch(w_node_in, rows=width, start=width),
+            Fetch(w_node_in, rows=width, start=2 * width, keep=True),
             Fetch(mesh_latents, rows=share, start=own_start, keep=True, defer=True),
             Fetch(cot_mesh, rows=share, start=own_start, keep=True, defer=True),
-            Fetch(w_node_in, keep=True, defer=True),
+            Fetch(w_node_in, rows=width, start=0, keep=True, defer=True),
             Fetch(w_node_out, keep=True, defer=True),
             Fetch(cot_edges, keep=True, defer=True),
+            Fetch(w_edge_in, rows=width, start=0, keep=True, defer=True),
+            Fetch(w_edge_in, rows=width, start=2 * width, keep=True, defer=True),
         ],
     )
     sums = swap(sums, "feat")
-    spread, new_share, own, w_first, w_last = call(
+    spread, new_share, own = call(
         node_kernel,
-        [((feats, share, width), BF), ((share, width), BF), Push((share, width), F32)],
-        [
-            sums,
-            mesh_own,
-            node_in,
-            node_out,
-            cot_own,
-            Fetch(w_edge_in, rows=width, start=0, keep=True),
-            Fetch(w_edge_in, rows=width, start=2 * width, keep=True),
-        ],
+        [((feats, share, width), BF), ((share, width), BF), ((share, width), F32)],
+        [sums, mesh_own, w_mesh, w_edge_sum, node_out, cot_own],
     )
     grads = swap(spread, "feat").reshape(nodes, width)
-    send, grad_edges, local, new_share = call(
+    send, grad_edges, local, new_share, own = call(
         functools.partial(edge_back_kernel, count=count),
         [
             Push((slots, back), BF),
             Push((edges, width), BF),
             Push((nodes, width), F32),
             Push((share, width), BF),
+            Push((share, width), F32),
         ],
         [
             grads,
@@ -526,6 +526,7 @@
             w_first,
             w_last,
             new_share,
+            own,
         ],
     )
     returned = swap(send.reshape(spaces, 8, back), "space").reshape(slots, back)

time: 162 us -> 155 us (0.957)
  blocking collectives: 90.5 us -> 84.7 us
    all_to_all x3, blocking collectives: 68.3 us -> 62.5 us  [swap(): return lax.all_to_all(values, axis, split_axis=0, concat_axis=0, tiled=True)]
where the time goes in v4:
time: 155 us
  blocking collectives  84.7 us (55%)
  waiting for transfers between devices  30.5 us (20%)
  starting transfers between devices  20.6 us (13%)
  Pallas kernels  16.9 us (11%)
    all_to_all x3, blocking collectives, swap(): return lax.all_to_all(values, axis, split_axis=0, concat_axis=0, tiled=True)  62.5 us
    all_to_all x2, waiting for transfers between devices, swap(): return lax.all_to_all(values, axis, split_axis=0, concat_axis=0, tiled=True)  30.5 us
    all_gather x1, blocking collectives, body(): new_mesh = lax.all_gather(new_share, 'feat', axis=0, tiled=True)  22.2 us
    all_to_all x2, starting transfers between devices, swap(): return lax.all_to_all(values, axis, split_axis=0, concat_axis=0, tiled=True)  20.6 us
    pallas_call x7, Pallas kernels, call(): pl.pallas_call(run, out_shape=out_shape + [pltpu.VMEM(arg.shape, arg.arra...  16.9 us
  transfers between devices with their start and end apart: 2, of which 1 were waited for; matrix products, arithmetic and copies ran while one was open for 1% of the time, Pallas kernels for 2%

profile of v4, /device:TPU:6, one launch (start us, length us, event | category | flops | bytes accessed | tf_op | source)
XLA Modules:
  0.0 154.6 jit_solution(9043656862034414736)
XLA Ops:
  0.6 3.5 %shard_map.174 = bf16[512,1408]{1,0:T(8,128)(2,1)} custom-call(s32[1,256]{1,0:T(1,128)} %bitcast.15, s32[1,256]{1,0:T(1,128)} %bitcast.16, s32[12,1,64]{2,1,0:T(1,128)} %bitcast.13, bf16[192,512]{1,0:T(8,128)(2,1)} %refs_10_.1, bf16[512,512]{1,0:T(8,128)(2,1)} %refs_4_.3, bf16[256,512]{1,0:T(8,128)(2,1)} %refs_5_.1), custom_call_target="tpu_custom_call" | custom-call | tf_op jit(solution)/shard_map/pallas_call | solution.py:145
  4.1 0.0 copy-start.1
  4.1 0.0 copy-start.2
  4.1 13.9 %all-to-all-start = ((bf16[64,8,1408]{2,1,0:T(8,128)(2,1)}), bf16[64,8,1408]{2,1,0:T(8,128)(2,1)S(1)}, u32[]{:S(2)}, u32[]{:S(2)}) async-start(bf16[64,8,1408]{2,1,0:T(8,128)(2,1)} %bitcast.11), calls=%async_computation | async-start | bytes 2883584 | tf_op jit(solution)/shard_map/all_to_all | solution.py:401
  18.1 0.0 copy-done.1
  18.1 0.6 reshape.39.refs_0_.refs_1_
  18.7 0.0 copy-done.2
  18.7 0.6 reshape.40.refs_1_.refs_2_
  19.2 3.3 %shard_map.175 = (f32[384,512]{1,0:T(8,128)}, bf16[384,512]{1,0:T(8,128)(2,1)}) custom-call(s32[1,384]{1,0:T(1,128)} %reshape.39.refs_0_.refs_1_, s32[1,384]{1,0:T(1,128)} %reshape.40.refs_1_.refs_2_, bf16[192,512]{1,0:T(8,128)(2,1)} %refs_10_.1, bf16[384,512]{1,0:T(8,128)(2,1)} %refs_7_.1, bf16[1536,512]{1,0:T(8,128)(2,1)} %refs_16_.1), custom_call_target="tpu_custom_call" | custom-call | tf_op jit(solution)/shard_map/pallas_call | solution.py:145
  22.5 30.5 %all-to-all-done = bf16[64,8,1408]{2,1,0:T(8,128)(2,1)S(1)} async-done(((bf16[64,8,1408]{2,1,0:T(8,128)(2,1)}), bf16[64,8,1408]{2,1,0:T(8,128)(2,1)S(1)}, u32[]{:S(2)}, u32[]{:S(2)}) %all-to-all-start) | async-done | bytes 1441824 | tf_op jit(solution)/shard_map/all_to_all | solution.py:401
  53.0 3.6 %shard_map.176 = (bf16[12,16,512]{2,1,0:T(8,128)(2,1)S(1)}, bf16[384,512]{1,0:T(8,128)(2,1)}, f32[384,512]{1,0:T(8,128)S(1)}, f32[384,512]{1,0:T(8,128)S(1)}, f3...) custom-call(bf16[512,1408]{1,0:T(8,128)(2,1)S(1)} %bitcast.8, ...), custom_call_target="tpu_custom_call" | custom-call | tf_op jit(solution)/shard_map/pallas_call | solution.py:145
  56.6 25.5 %all_to_all.25.refs_0_ = bf16[12,16,512]{2,1,0:T(8,128)(2,1)S(1)} all-to-all(bf16[12,16,512]{2,1,0:T(8,128)(2,1)S(1)} %get-tuple-element.36), channel_id=1, replica_groups=mesh['space'=64,'feat'=12] {'feat'}, dimensions={0} | all-to-all | bytes 393216 | tf_op jit(solution)/shard_map/all_to_all | solution.py:401
  82.2 1.1 shard_map.177
  83.3 19.0 %all_to_all.26 = bf16[12,16,512]{2,1,0:T(8,128)(2,1)S(1)} all-to-all(bf16[12,16,512]{2,1,0:T(8,128)(2,1)S(1)} %get-tuple-element.42), channel_id=1, replica_groups=mesh['space'=64,'feat'=12] {'feat'}, dimensions={0} | all-to-all | bytes 393216 | tf_op jit(solution)/shard_map/all_to_all | solution.py:401
  102.3 3.5 %shard_map.178 = (bf16[512,768]{1,0:T(8,128)(2,1)}, bf16[384,512]{1,0:T(8,128)(2,1)}, f32[192,512]{1,0:T(8,128)}, bf16[16,512]{1,0:T(8,128)(2,1)}, f32[16,512]{1,0:T(8,128)}) custom-call(bf16[192,512]{1,0:T(8,128)(2,1)S(1)} %bitcast.10, bf16[384,512]{1,0:T(8,128)(2,1)S(1)} %get-tuple-element.43.refs_1_, bf16[512,512]{1,0:T(8,128)(2,1)S(1)} %get-tuple-element.44.refs_2_, ...), custom_call_target="tpu_custom_call" | custom-call | tf_op jit(solution)/shard_map/pallas_call | solution.py:145
  105.7 0.0 copy-start
  105.7 6.7 %all-to-all-start.3 = ((bf16[64,8,768]{2,1,0:T(8,128)(2,1)}), bf16[64,8,768]{2,1,0:T(8,128)(2,1)S(1)}, u32[]{:S(2)}, u32[]{:S(2)}) async-start(bf16[64,8,768]{2,1,0:T(8,128)(2,1)} %bitcast.12), calls=%async_computation.3 | async-start | bytes 1572864 | tf_op jit(solution)/shard_map/all_to_all | solution.py:401
  112.5 0.0 copy-done
  112.5 22.2 %all_gather.3.refs_4_ = bf16[192,512]{1,0:T(8,128)(2,1)S(1)} all-gather(bf16[16,512]{1,0:T(8,128)(2,1)S(1)} %copy-done), channel_id=1, replica_groups=mesh['space'=64,'feat'=12] {'feat'}, dimensions={0}, use_global_device_ids=true | all-gather | bytes 212992 | tf_op jit(solution)/shard_map/all_gather | solution.py:533
  134.7 0.0 all-to-all-done.3
  134.7 1.3 shard_map.179
  135.9 18.0 %all_to_all.27.refs_0_ = bf16[12,16,512]{2,1,0:T(8,128)(2,1)S(1)} all-to-all(bf16[12,16,512]{2,1,0:T(8,128)(2,1)S(1)} %get-tuple-element.61), channel_id=1, replica_groups=mesh['space'=64,'feat'=12] {'feat'}, dimensions={0} | all-to-all | bytes 393216 | tf_op jit(solution)/shard_map/all_to_all | solution.py:401
  153.9 0.7 shard_map.180
Async XLA Ops:
  4.1 14.0 %copy-start.1 = (s32[384]{0:T(512)S(1)}, s32[384]{0:T(512)}, u32[]{:S(2)}) copy-start(s32[384]{0:T(512)} %param.20) | copy-start | bytes 4612
  4.1 14.5 %copy-start.2 = (s32[384]{0:T(512)S(1)}, s32[384]{0:T(512)}, u32[]{:S(2)}) copy-start(s32[384]{0:T(512)} %param.21) | copy-start | bytes 4612
  4.1 48.8 %all-to-all-start = ((bf16[64,8,1408]{2,1,0:T(8,128)(2,1)}), bf16[64,8,1408]{2,1,0:T(8,128)(2,1)S(1)}, u32[]{:S(2)}, u32[]{:S(2)}) async-start(bf16[64,8,1408]{2,1,0:T(8,128)(2,1)} %bitcast.11), calls=%async_computation | async-start | bytes 2883584 | tf_op jit(solution)/shard_map/all_to_all | solution.py:401
  105.7 6.7 %copy-start = (bf16[16,512]{1,0:T(8,128)(2,1)S(1)}, bf16[16,512]{1,0:T(8,128)(2,1)}, u32[]{:S(2)}) copy-start(bf16[16,512]{1,0:T(8,128)(2,1)} %get-tuple-element.58) | copy-start | bytes 49156
  105.7 28.9 %all-to-all-start.3 = ((bf16[64,8,768]{2,1,0:T(8,128)(2,1)}), bf16[64,8,768]{2,1,0:T(8,128)(2,1)S(1)}, u32[]{:S(2)}, u32[]{:S(2)}) async-start(bf16[64,8,768]{2,1,0:T(8,128)(2,1)} %bitcast.12), calls=%async_computation.3 | async-start | bytes 1572864 | tf_op jit(solution)/shard_map/all_to_all | solution.py:401

commit v5 on v4

--- a/solution.py
+++ b/solution.py
@@ -185,7 +185,21 @@
     return v * s, s * (1.0 + v * (1.0 - s))
 
 
-def pack_kernel(region_ref, node_ref, halo_ref, mesh_ref, w_ref, grid_ref, out_ref):
+def pack_kernel(
+    region_ref,
+    node_ref,
+    halo_ref,
+    mesh_ref,
+    w_ref,
+    grid_ref,
+    sender_ref,
+    receiver_ref,
+    edge_ref,
+    w_in_ref,
+    w_out_ref,
+    w_sums_ref,
+    out_ref,
+):
     rows, width = grid_ref.shape
     half = width // 2
     spaces = halo_ref.shape[2]
@@ -198,21 +212,20 @@
     place = iota((slots, rows), 0) == region * 8 + rank
     label = (node_ref[...] + 1).astype(F32)
     labels = jnp.sum(jnp.where(place, label, 0.0), axis=1, keepdims=True)
-    wide = out_ref.shape[1]
-    out_ref.put(jnp.broadcast_to(labels, (slots, 128)).astype(BF), 2 * width + half, wide)
+    out_ref[:, 2 * width + half :] = jnp.broadcast_to(labels, (slots, 128)).astype(BF)
     halo_t = halo_ref[...].reshape(halo_ref.shape[0], spaces)
     first = halo_column(halo_t, 8, 0)
     rest = halo_column(halo_t, 4, 8)
     mesh = mesh_ref[...]
     ids = iota((slots, mesh.shape[0]), 1)
-    out_ref.put(mm(one_hot(first, ids), mesh).astype(BF), 0, width)
+    out_ref[:, :width] = mm(one_hot(first, ids), mesh).astype(BF)
     tail = mm(one_hot(rest, ids), mesh)
     left = iota((slots, half), 0) % 8 < 4
     tail = jnp.where(left, tail[:, :half], tail[:, half:]).astype(BF)
-    out_ref.put(tail, width, width + half)
+    out_ref[:, width : width + half] = tail
     message = silu_parts(mm(grid_ref[...], w_ref[...]))[0].astype(BF)
     placed = mm(place.astype(F32).astype(BF), message).astype(BF)
-    out_ref.put(placed, width + half, 2 * width + half)
+    out_ref[:, width + half : 2 * width + half] = placed
 
 
 def table_ids(shape, dim, nodes, count):
@@ -223,35 +236,20 @@
     return base + j, jnp.where(j < 4, tail, -1), jnp.where(j < 4, -1, tail)
 
 
-def ready_kernel(sender_ref, receiver_ref, mesh_ref, edge_ref, w_in_ref, base_ref, local_ref):
-    edges, width = edge_ref.shape
-    nodes = mesh_ref.shape[0]
-    ids = iota((edges, nodes), 1)
-    mesh = mesh_ref[...]
-    receiver_rows = mm(one_hot(column_of(receiver_ref[...]), ids), mesh).astype(BF)
-    local_ref.put(mm(one_hot(column_of(sender_ref[...]), ids), mesh).astype(BF))
-    base = mm(edge_ref[...], w_in_ref[:width, :])
-    base_ref.put(base + mm(receiver_rows, w_in_ref[2 * width :, :]))
-
-
 def edge_forward_kernel(
     got_ref,
     sender_ref,
     receiver_ref,
-    local_ref,
-    w_mid_ref,
-    base_ref,
+    mesh_ref,
+    w_in_ref,
     w_out_ref,
     edge_ref,
-    w_grid_sum_ref,
-    w_edge_sum_ref,
-    mesh_ref,
+    w_sums_ref,
+    mesh_own_ref,
     cot_ref,
     w_mesh_ref,
     node_out_ref,
     cot_edges_ref,
-    w_first_ref,
-    w_last_ref,
     sums_ref,
     new_ref,
     slope_ref,
@@ -264,21 +262,18 @@
     slots = got_ref.shape[0]
     feats, share, _ = sums_ref.shape
     nodes = feats * share
-    label = got_ref[:, 2 * width + half :].astype(F32).T[0:1, :].astype(jnp.int32)
-    grid_sum = mm(
-        one_hot(iota((nodes, slots), 0) + 1, label), got_ref[:, width + half : 2 * width + half]
-    ).astype(BF)
-    sender = column_of(sender_ref[...])
+    receiver_row = receiver_ref[...].reshape(1, edges)
+    sender = column_of(sender_ref[...].reshape(1, edges))
     whole, left, right = table_ids((1, slots), 1, nodes, count)
+    mesh = mesh_ref[...]
+    ids = iota((edges, nodes), 1)
+    receiver_rows = mm(one_hot(column_of(receiver_row), ids), mesh).astype(BF)
     head = mm(one_hot(sender, whole), got_ref[:, :width])
     tail = got_ref[:, width : width + half]
     tails = [mm(one_hot(sender, left), tail), mm(one_hot(sender, right), tail)]
-    for later in (mesh_ref, cot_ref, w_mesh_ref, node_out_ref, cot_edges_ref):
-        later.start()
-    w_first_ref.start()
-    w_last_ref.start()
-    head = head + jnp.concatenate(tails, 1) + local_ref[...].astype(F32)
-    v = mm(head.astype(BF), w_mid_ref[...]) + base_ref[...]
+    head = head + jnp.concatenate(tails, 1) + mm(one_hot(sender, ids), mesh)
+    v = mm(edge_ref[...], w_in_ref[:width, :]) + mm(receiver_rows, w_in_ref[2 * width :, :])
+    v = v + mm(head.astype(BF), w_in_ref[width : 2 * width, :])
     act, slope = silu_parts(v)
     slope_ref[...] = slope
     u = mm(act.astype(BF), w_out_ref[...])
@@ -289,9 +284,13 @@
     rstd_ref[...] = jnp.broadcast_to(rstd, rstd_ref.shape)
     new = (edge_ref[...].astype(F32) + xhat).astype(BF)
     new_ref.put(new)
-    to_receiver = one_hot(iota((nodes, edges), 0), receiver_ref[...])
+    to_receiver = one_hot(iota((nodes, edges), 0), receiver_row)
+    label = got_ref[:, 2 * width + half :].astype(F32).T[0:1, :].astype(jnp.int32)
+    grid_sum = mm(
+        one_hot(iota((nodes, slots), 0) + 1, label), got_ref[:, width + half : 2 * width + half]
+    ).astype(BF)
     edge_sum = mm(to_receiver, new).astype(BF)
-    terms = mm(grid_sum, w_grid_sum_ref[...]) + mm(edge_sum, w_edge_sum_ref[...])
+    terms = mm(grid_sum, w_sums_ref[:width, :]) + mm(edge_sum, w_sums_ref[width:, :])
     sums_ref[...] = terms.astype(BF).reshape(feats, share, width)
 
 
@@ -299,7 +298,7 @@
     sums_ref,
     mesh_ref,
     w_mesh_ref,
-    w_edge_sum_ref,
+    w_sums_ref,
     w_out_ref,
     cot_ref,
     spread_ref,
@@ -318,7 +317,7 @@
     du = norm_back(cot, xhat, rstd)
     dh = mm_nt(du.astype(BF), w_out_ref[...]).astype(BF)
     dv = (dh.astype(F32) * slope).astype(BF)
-    sum_grad = mm_nt(dv, w_edge_sum_ref[...]).astype(BF)
+    sum_grad = mm_nt(dv, w_sums_ref[w_out_ref.shape[0] :, :]).astype(BF)
     spread_ref[...] = jnp.broadcast_to(sum_grad[None], spread_ref.shape)
     own_ref[...] = cot + mm_nt(dv, w_mesh_ref[...]).astype(BF).astype(F32)
 
@@ -335,14 +334,12 @@
     grads_ref,
     cot_ref,
     w_out_ref,
-    w_mid_ref,
+    w_in_ref,
     sender_ref,
     receiver_ref,
     xhat_ref,
     rstd_ref,
     slope_ref,
-    w_first_ref,
-    w_last_ref,
     new_ref,
     own_ref,
     send_ref,
@@ -358,22 +355,23 @@
     half = width // 2
     nodes = grads_ref.shape[0]
     slots = send_ref.shape[0]
-    sender, receiver = sender_ref[...], receiver_ref[...]
+    sender = sender_ref[...].reshape(1, edges)
+    receiver = receiver_ref[...].reshape(1, edges)
     spread = mm(one_hot(column_of(receiver), iota((edges, nodes), 1)), grads_ref[...])
     cot = (cot_ref[...].astype(F32) + spread).astype(BF)
     du = norm_back(cot.astype(F32), xhat_ref[...], rstd_ref[:, 0:1])
     dh = mm_nt(du.astype(BF), w_out_ref[...]).astype(BF)
     dv = (dh.astype(F32) * slope_ref[...]).astype(BF)
-    sgrad = mm_nt(dv, w_mid_ref[...]).astype(BF)
+    sgrad = mm_nt(dv, w_in_ref[width : 2 * width, :]).astype(BF)
     whole, left, right = table_ids((slots, 1), 0, nodes, count)
     send_ref.put(mm(one_hot(whole, sender), sgrad).astype(BF), 0, width)
     tail = mm(one_hot(jnp.maximum(left, right), sender), sgrad)
     tail = jnp.where(left >= 0, tail[:, :half], tail[:, half:]).astype(BF)
     send_ref.put(tail, width, width + half)
-    rgrad = mm_nt(dv, w_last_ref[...]).astype(BF)
+    rgrad = mm_nt(dv, w_in_ref[2 * width :, :]).astype(BF)
     ids = iota((nodes, edges), 0)
     local_ref.put(mm(one_hot(ids, sender), sgrad) + mm(one_hot(ids, receiver), rgrad))
-    direct = mm_nt(dv, w_first_ref[...]).astype(BF)
+    direct = mm_nt(dv, w_in_ref[:width, :]).astype(BF)
     grad_ref.put((cot.astype(F32) + direct.astype(F32)).astype(BF))
 
 
@@ -428,46 +426,42 @@
     back = width + width // 2
     region_row = grid_region.reshape(1, -1)
     node_row = grid_node.reshape(1, -1)
-    sender = edge_sender.reshape(1, -1)
-    receiver = edge_receiver.reshape(1, -1)
     halo_t = halo_send.transpose(2, 0, 1)
     wide = 2 * width + width // 2 + 128
 
     def own_start():
         return pl.multiple_of(lax.axis_index("feat") * share, share)
 
-    (packed,) = call(
+    packed, mesh, sender, receiver, edge, w_in, w_out, w_sums = call(
         pack_kernel,
-        [Push((slots, wide), BF)],
+        [((slots, wide), BF)],
         [
-            Fetch(array)
-            for array in (region_row, node_row, halo_t, mesh_latents, w_grid, grid_latents)
+            Fetch(region_row),
+            Fetch(node_row),
+            Fetch(halo_t),
+            Fetch(mesh_latents, keep=True),
+            Fetch(w_grid),
+            Fetch(grid_latents),
+            Fetch(edge_sender, keep=True),
+            Fetch(edge_receiver, keep=True),
+            Fetch(edge_latents, keep=True),
+            Fetch(w_edge_in, keep=True),
+            Fetch(w_edge_out, keep=True),
+            Fetch(w_node_in, rows=2 * width, start=width, keep=True),
         ],
     )
     got = swap(packed.reshape(spaces, 8, wide), "space").reshape(slots, wide)
-    base, sender_local = call(
-        ready_kernel,
-        [Push((edges, width), F32), Push((edges, width), BF)],
-        [Fetch(array) for array in (sender, receiver, mesh_latents, edge_latents, w_edge_in)],
-    )
     (
         sums,
         new_edges,
         slope,
         xhat,
         rstd,
-        sender_held,
-        receiver_held,
-        w_mid,
-        w_out,
-        w_edge_sum,
         mesh_own,
         cot_own,
         w_mesh,
         node_out,
         edge_cot,
-        w_first,
-        w_last,
     ) = call(
         functools.partial(edge_forward_kernel, count=count),
         [
@@ -479,29 +473,25 @@
         ],
         [
             got,
-            Fetch(sender, keep=True),
-            Fetch(receiver, keep=True),
-            Fetch(sender_local),
-            Fetch(w_edge_in, rows=width, start=width, keep=True),
-            Fetch(base),
-            Fetch(w_edge_out, keep=True),
-            Fetch(edge_latents),
-            Fetch(w_node_in, rows=width, start=width),
-            Fetch(w_node_in, rows=width, start=2 * width, keep=True),
-            Fetch(mesh_latents, rows=share, start=own_start, keep=True, defer=True),
-            Fetch(cot_mesh, rows=share, start=own_start, keep=True, defer=True),
-            Fetch(w_node_in, rows=width, start=0, keep=True, defer=True),
-            Fetch(w_node_out, keep=True, defer=True),
-            Fetch(cot_edges, keep=True, defer=True),
-            Fetch(w_edge_in, rows=width, start=0, keep=True, defer=True),
-            Fetch(w_edge_in, rows=width, start=2 * width, keep=True, defer=True),
+            sender,
+            receiver,
+            mesh,
+            w_in,
+            w_out,
+            edge,
+            w_sums,
+            Fetch(mesh_latents, rows=share, start=own_start, keep=True),
+            Fetch(cot_mesh, rows=share, start=own_start, keep=True),
+            Fetch(w_node_in, rows=width, start=0, keep=True),
+            Fetch(w_node_out, keep=True),
+            Fetch(cot_edges, keep=True),
         ],
     )
     sums = swap(sums, "feat")
     spread, new_share, own = call(
         node_kernel,
         [((feats, share, width), BF), ((share, width), BF), ((share, width), F32)],
-        [sums, mesh_own, w_mesh, w_edge_sum, node_out, cot_own],
+        [sums, mesh_own, w_mesh, w_sums, node_out, cot_own],
     )
     grads = swap(spread, "feat").reshape(nodes, width)
     send, grad_edges, local, new_share, own = call(
@@ -517,14 +507,12 @@
             grads,
             edge_cot,
             w_out,
-            w_mid,
-            sender_held,
-            receiver_held,
+            w_in,
+            sender,
+            receiver,
             xhat,
             rstd,
             slope,
-            w_first,
-            w_last,
             new_share,
             own,
         ],

time: 155 us -> 155 us (level)
  blocking collectives: 84.7 us -> 133 us
  waiting for transfers between devices: 30.5 us -> 0.01 us
  starting transfers between devices: 20.6 us -> 6.71 us
  Pallas kernels: 16.9 us -> 13.3 us
    all_to_all x3 -> x4, blocking collectives: 62.5 us -> 111 us  [swap(): return lax.all_to_all(values, axis, split_axis=0, concat_axis=0, tiled=True)]
    all_to_all x2 -> x1, waiting for transfers between devices: 30.5 us -> 0.01 us  [swap(): return lax.all_to_all(values, axis, split_axis=0, concat_axis=0, tiled=True)]
    all_to_all x2 -> x1, starting transfers between devices: 20.6 us -> 6.71 us  [swap(): return lax.all_to_all(values, axis, split_axis=0, concat_axis=0, tiled=True)]
    pallas_call x7 -> x6, Pallas kernels: 16.9 us -> 13.3 us  [call(): pl.pallas_call(run, out_shape=out_shape + [pltpu.VMEM(arg.shape, arg.arra...]
  transfers between devices with their start and end apart: 2 -> 1, of which waited for: 1 -> 0; matrix products, arithmetic and copies ran while one was open for 1% -> 0% of each run, Pallas kernels for 2% -> 0%
where the time goes in v5:
time: 155 us; the launch traced here: 154 us
  blocking collectives  133 us (86%)
  Pallas kernels  13.3 us (9%)
  starting transfers between devices  6.71 us (4%)
    all_to_all x4, blocking collectives, swap(): return lax.all_to_all(values, axis, split_axis=0, concat_axis=0, tiled=True)  111 us
    all_gather x1, blocking collectives, body(): new_mesh = lax.all_gather(new_share, 'feat', axis=0, tiled=True)  22.2 us
    pallas_call x6, Pallas kernels, call(): pl.pallas_call(run, out_shape=out_shape + [pltpu.VMEM(arg.shape, arg.arra...  13.3 us
    all_to_all x1, starting transfers between devices, swap(): return lax.all_to_all(values, axis, split_axis=0, concat_axis=0, tiled=True)  6.71 us
  transfers between devices with their start and end apart: 1, of which 0 were waited for; matrix products, arithmetic and copies ran while one was open for 0% of the time, Pallas kernels for 0%

profile of v5, /device:TPU:6, one launch (start us, length us, event | category | flops | bytes accessed | tf_op | source)
XLA Modules:
  0.0 154.0 jit_solution(1765289542427112677)
XLA Ops:
  0.6 2.6 %shard_map.174 = (bf16[512,1408]{1,0:T(8,128)(2,1)S(1)}, bf16[192,512]{1,0:T(8,128)(2,1)S(1)}, s32[384]{0:T(512)S(1)}, s32[384]{0:T(512)S(1)}, bf16[384,512]{1,0...) custom-call(s32[1,256]{1,0:T(1,128)} %bitcast.15, ...), custom_call_target="tpu_custom_call" | custom-call | tf_op jit(solution)/shard_map/pallas_call | solution.py:145
  3.3 48.0 %all_to_all.25 = bf16[64,8,1408]{2,1,0:T(8,128)(2,1)S(1)} all-to-all(bf16[64,8,1408]{2,1,0:T(8,128)(2,1)S(1)} %bitcast.10), channel_id=1, replica_groups=mesh['space'=64,'feat'=12] {'space'}, dimensions={0} | all-to-all | bytes 2883584 | tf_op jit(solution)/shard_map/all_to_all | solution.py:399
  51.3 4.1 %shard_map.175 = (bf16[12,16,512]{2,1,0:T(8,128)(2,1)S(1)}, bf16[384,512]{1,0:T(8,128)(2,1)}, f32[384,512]{1,0:T(8,128)S(1)}, f32[384,512]{1,0:T(8,128)S(1)}, f3...) custom-call(bf16[512,1408]{1,0:T(8,128)(2,1)S(1)} %bitcast.8, ...), custom_call_target="tpu_custom_call" | custom-call | tf_op jit(solution)/shard_map/pallas_call | solution.py:145
  55.4 26.2 %all_to_all.26.refs_0_ = bf16[12,16,512]{2,1,0:T(8,128)(2,1)S(1)} all-to-all(bf16[12,16,512]{2,1,0:T(8,128)(2,1)S(1)} %get-tuple-element.41), channel_id=1, replica_groups=mesh['space'=64,'feat'=12] {'feat'}, dimensions={0} | all-to-all | bytes 393216 | tf_op jit(solution)/shard_map/all_to_all | solution.py:399
  81.5 1.1 shard_map.176
  82.6 19.0 %all_to_all.27 = bf16[12,16,512]{2,1,0:T(8,128)(2,1)S(1)} all-to-all(bf16[12,16,512]{2,1,0:T(8,128)(2,1)S(1)} %get-tuple-element.46), channel_id=1, replica_groups=mesh['space'=64,'feat'=12] {'feat'}, dimensions={0} | all-to-all | bytes 393216 | tf_op jit(solution)/shard_map/all_to_all | solution.py:399
  101.6 3.5 %shard_map.177 = (bf16[512,768]{1,0:T(8,128)(2,1)}, bf16[384,512]{1,0:T(8,128)(2,1)}, f32[192,512]{1,0:T(8,128)}, bf16[16,512]{1,0:T(8,128)(2,1)}, f32[16,512]{1,0:T(8,128)}) custom-call(bf16[192,512]{1,0:T(8,128)(2,1)S(1)} %bitcast.11, bf16[384,512]{1,0:T(8,128)(2,1)S(1)} %get-tuple-element.47.refs_1_, ...), custom_call_target="tpu_custom_call" | custom-call | tf_op jit(solution)/shard_map/pallas_call | solution.py:145
  105.1 0.0 copy-start
  105.1 6.7 %all-to-all-start.3 = ((bf16[64,8,768]{2,1,0:T(8,128)(2,1)}), bf16[64,8,768]{2,1,0:T(8,128)(2,1)S(1)}, u32[]{:S(2)}, u32[]{:S(2)}) async-start(bf16[64,8,768]{2,1,0:T(8,128)(2,1)} %bitcast.12), calls=%async_computation.3 | async-start | bytes 1572864 | tf_op jit(solution)/shard_map/all_to_all | solution.py:399
  111.9 0.0 copy-done
  111.9 22.2 %all_gather.3.refs_4_ = bf16[192,512]{1,0:T(8,128)(2,1)S(1)} all-gather(bf16[16,512]{1,0:T(8,128)(2,1)S(1)} %copy-done), channel_id=1, replica_groups=mesh['space'=64,'feat'=12] {'feat'}, dimensions={0}, use_global_device_ids=true | all-gather | bytes 212992 | tf_op jit(solution)/shard_map/all_gather | solution.py:521
  134.0 0.0 all-to-all-done.3
  134.0 1.3 shard_map.178
  135.3 18.0 %all_to_all.28.refs_0_ = bf16[12,16,512]{2,1,0:T(8,128)(2,1)S(1)} all-to-all(bf16[12,16,512]{2,1,0:T(8,128)(2,1)S(1)} %get-tuple-element.59), channel_id=1, replica_groups=mesh['space'=64,'feat'=12] {'feat'}, dimensions={0} | all-to-all | bytes 393216 | tf_op jit(solution)/shard_map/all_to_all | solution.py:399
  153.3 0.7 shard_map.179
Async XLA Ops:
  105.1 6.7 %copy-start = (bf16[16,512]{1,0:T(8,128)(2,1)S(1)}, bf16[16,512]{1,0:T(8,128)(2,1)}, u32[]{:S(2)}) copy-start(bf16[16,512]{1,0:T(8,128)(2,1)} %get-tuple-element.56) | copy-start | bytes 49156
  105.1 28.9 %all-to-all-start.3 = ((bf16[64,8,768]{2,1,0:T(8,128)(2,1)}), bf16[64,8,768]{2,1,0:T(8,128)(2,1)S(1)}, u32[]{:S(2)}, u32[]{:S(2)}) async-start(bf16[64,8,768]{2,1,0:T(8,128)(2,1)} %bitcast.12), calls=%async_computation.3 | async-start | bytes 1572864 | tf_op jit(solution)/shard_map/all_to_all | solution.py:399

commit v6 on v4

--- a/solution.py
+++ b/solution.py
@@ -365,6 +365,8 @@
     dh = mm_nt(du.astype(BF), w_out_ref[...]).astype(BF)
     dv = (dh.astype(F32) * slope_ref[...]).astype(BF)
     sgrad = mm_nt(dv, w_mid_ref[...]).astype(BF)
+    direct = mm_nt(dv, w_first_ref[...]).astype(BF)
+    grad_ref.put((cot.astype(F32) + direct.astype(F32)).astype(BF))
     whole, left, right = table_ids((slots, 1), 0, nodes, count)
     send_ref.put(mm(one_hot(whole, sender), sgrad).astype(BF), 0, width)
     tail = mm(one_hot(jnp.maximum(left, right), sender), sgrad)
@@ -373,8 +375,6 @@
     rgrad = mm_nt(dv, w_last_ref[...]).astype(BF)
     ids = iota((nodes, edges), 0)
     local_ref.put(mm(one_hot(ids, sender), sgrad) + mm(one_hot(ids, receiver), rgrad))
-    direct = mm_nt(dv, w_first_ref[...]).astype(BF)
-    grad_ref.put((cot.astype(F32) + direct.astype(F32)).astype(BF))
 
 
 def return_kernel(got_ref, halo_ref, local_ref, own_ref, new_ref, out_ref, new_out_ref):

time: 155 us -> 155 us (level)
  no operation moved by 1% of the time
where the time goes in v6:
time: 155 us; the launch traced here: 154 us
  blocking collectives  84.7 us (55%)
  waiting for transfers between devices  30.5 us (20%)
  starting transfers between devices  20.6 us (13%)
  Pallas kernels  16.8 us (11%)
    all_to_all x3, blocking collectives, swap(): return lax.all_to_all(values, axis, split_axis=0, concat_axis=0, tiled=True)  62.5 us
    all_to_all x2, waiting for transfers between devices, swap(): return lax.all_to_all(values, axis, split_axis=0, concat_axis=0, tiled=True)  30.5 us
    all_gather x1, blocking collectives, body(): new_mesh = lax.all_gather(new_share, 'feat', axis=0, tiled=True)  22.2 us
    all_to_all x2, starting transfers between devices, swap(): return lax.all_to_all(values, axis, split_axis=0, concat_axis=0, tiled=True)  20.6 us
    pallas_call x7, Pallas kernels, call(): pl.pallas_call(run, out_shape=out_shape + [pltpu.VMEM(arg.shape, arg.arra...  16.8 us
  transfers between devices with their start and end apart: 2, of which 1 were waited for; matrix products, arithmetic and copies ran while one was open for 1% of the time, Pallas kernels for 2%

profile of v6, /device:TPU:6, one launch (start us, length us, event | category | flops | bytes accessed | tf_op | source)
XLA Modules:
  0.0 154.4 jit_solution(12404822883236282290)
XLA Ops:
  0.6 3.5 %shard_map.174 = bf16[512,1408]{1,0:T(8,128)(2,1)} custom-call(s32[1,256]{1,0:T(1,128)} %bitcast.15, s32[1,256]{1,0:T(1,128)} %bitcast.16, s32[12,1,64]{2,1,0:T(1,128)} %bitcast.13, bf16[192,512]{1,0:T(8,128)(2,1)} %refs_10_.1, bf16[512,512]{1,0:T(8,128)(2,1)} %refs_4_.3, bf16[256,512]{1,0:T(8,128)(2,1)} %refs_5_.1), custom_call_target="tpu_custom_call" | custom-call | tf_op jit(solution)/shard_map/pallas_call | solution.py:145
  4.1 0.0 copy-start.1
  4.1 0.0 copy-start.2
  4.1 13.9 %all-to-all-start = ((bf16[64,8,1408]{2,1,0:T(8,128)(2,1)}), bf16[64,8,1408]{2,1,0:T(8,128)(2,1)S(1)}, u32[]{:S(2)}, u32[]{:S(2)}) async-start(bf16[64,8,1408]{2,1,0:T(8,128)(2,1)} %bitcast.11), calls=%async_computation | async-start | bytes 2883584 | tf_op jit(solution)/shard_map/all_to_all | solution.py:401
  18.1 0.0 copy-done.1
  18.1 0.6 reshape.39.refs_0_.refs_1_
  18.7 0.0 copy-done.2
  18.7 0.6 reshape.40.refs_1_.refs_2_
  19.2 3.3 %shard_map.175 = (f32[384,512]{1,0:T(8,128)}, bf16[384,512]{1,0:T(8,128)(2,1)}) custom-call(s32[1,384]{1,0:T(1,128)} %reshape.39.refs_0_.refs_1_, s32[1,384]{1,0:T(1,128)} %reshape.40.refs_1_.refs_2_, bf16[192,512]{1,0:T(8,128)(2,1)} %refs_10_.1, bf16[384,512]{1,0:T(8,128)(2,1)} %refs_7_.1, bf16[1536,512]{1,0:T(8,128)(2,1)} %refs_16_.1), custom_call_target="tpu_custom_call" | custom-call | tf_op jit(solution)/shard_map/pallas_call | solution.py:145
  22.5 30.5 %all-to-all-done = bf16[64,8,1408]{2,1,0:T(8,128)(2,1)S(1)} async-done(((bf16[64,8,1408]{2,1,0:T(8,128)(2,1)}), bf16[64,8,1408]{2,1,0:T(8,128)(2,1)S(1)}, u32[]{:S(2)}, u32[]{:S(2)}) %all-to-all-start) | async-done | bytes 1441824 | tf_op jit(solution)/shard_map/all_to_all | solution.py:401
  53.0 3.6 %shard_map.176 = (bf16[12,16,512]{2,1,0:T(8,128)(2,1)S(1)}, bf16[384,512]{1,0:T(8,128)(2,1)}, f32[384,512]{1,0:T(8,128)S(1)}, f32[384,512]{1,0:T(8,128)S(1)}, f3...) custom-call(bf16[512,1408]{1,0:T(8,128)(2,1)S(1)} %bitcast.8, ...), custom_call_target="tpu_custom_call" | custom-call | tf_op jit(solution)/shard_map/pallas_call | solution.py:145
  56.6 25.5 %all_to_all.25.refs_0_ = bf16[12,16,512]{2,1,0:T(8,128)(2,1)S(1)} all-to-all(bf16[12,16,512]{2,1,0:T(8,128)(2,1)S(1)} %get-tuple-element.36), channel_id=1, replica_groups=mesh['space'=64,'feat'=12] {'feat'}, dimensions={0} | all-to-all | bytes 393216 | tf_op jit(solution)/shard_map/all_to_all | solution.py:401
  82.2 1.1 shard_map.177
  83.3 19.0 %all_to_all.26 = bf16[12,16,512]{2,1,0:T(8,128)(2,1)S(1)} all-to-all(bf16[12,16,512]{2,1,0:T(8,128)(2,1)S(1)} %get-tuple-element.42), channel_id=1, replica_groups=mesh['space'=64,'feat'=12] {'feat'}, dimensions={0} | all-to-all | bytes 393216 | tf_op jit(solution)/shard_map/all_to_all | solution.py:401
  102.3 3.3 %shard_map.178 = (bf16[512,768]{1,0:T(8,128)(2,1)}, bf16[384,512]{1,0:T(8,128)(2,1)}, f32[192,512]{1,0:T(8,128)}, bf16[16,512]{1,0:T(8,128)(2,1)}, f32[16,512]{1,0:T(8,128)}) custom-call(bf16[192,512]{1,0:T(8,128)(2,1)S(1)} %bitcast.10, bf16[384,512]{1,0:T(8,128)(2,1)S(1)} %get-tuple-element.43.refs_1_, bf16[512,512]{1,0:T(8,128)(2,1)S(1)} %get-tuple-element.44.refs_2_, ...), custom_call_target="tpu_custom_call" | custom-call | tf_op jit(solution)/shard_map/pallas_call | solution.py:145
  105.6 0.0 copy-start
  105.6 6.7 %all-to-all-start.3 = ((bf16[64,8,768]{2,1,0:T(8,128)(2,1)}), bf16[64,8,768]{2,1,0:T(8,128)(2,1)S(1)}, u32[]{:S(2)}, u32[]{:S(2)}) async-start(bf16[64,8,768]{2,1,0:T(8,128)(2,1)} %bitcast.12), calls=%async_computation.3 | async-start | bytes 1572864 | tf_op jit(solution)/shard_map/all_to_all | solution.py:401
  112.3 0.0 copy-done
  112.3 22.2 %all_gather.3.refs_4_ = bf16[192,512]{1,0:T(8,128)(2,1)S(1)} all-gather(bf16[16,512]{1,0:T(8,128)(2,1)S(1)} %copy-done), channel_id=1, replica_groups=mesh['space'=64,'feat'=12] {'feat'}, dimensions={0}, use_global_device_ids=true | all-gather | bytes 212992 | tf_op jit(solution)/shard_map/all_gather | solution.py:533
  134.5 0.0 all-to-all-done.3
  134.5 1.3 shard_map.179
  135.8 18.0 %all_to_all.27.refs_0_ = bf16[12,16,512]{2,1,0:T(8,128)(2,1)S(1)} all-to-all(bf16[12,16,512]{2,1,0:T(8,128)(2,1)S(1)} %get-tuple-element.61), channel_id=1, replica_groups=mesh['space'=64,'feat'=12] {'feat'}, dimensions={0} | all-to-all | bytes 393216 | tf_op jit(solution)/shard_map/all_to_all | solution.py:401
  153.8 0.7 shard_map.180
Async XLA Ops:
  4.1 14.0 %copy-start.1 = (s32[384]{0:T(512)S(1)}, s32[384]{0:T(512)}, u32[]{:S(2)}) copy-start(s32[384]{0:T(512)} %param.20) | copy-start | bytes 4612
  4.1 14.5 %copy-start.2 = (s32[384]{0:T(512)S(1)}, s32[384]{0:T(512)}, u32[]{:S(2)}) copy-start(s32[384]{0:T(512)} %param.21) | copy-start | bytes 4612
  4.1 48.8 %all-to-all-start = ((bf16[64,8,1408]{2,1,0:T(8,128)(2,1)}), bf16[64,8,1408]{2,1,0:T(8,128)(2,1)S(1)}, u32[]{:S(2)}, u32[]{:S(2)}) async-start(bf16[64,8,1408]{2,1,0:T(8,128)(2,1)} %bitcast.11), calls=%async_computation | async-start | bytes 2883584 | tf_op jit(solution)/shard_map/all_to_all | solution.py:401
  105.6 6.7 %copy-start = (bf16[16,512]{1,0:T(8,128)(2,1)S(1)}, bf16[16,512]{1,0:T(8,128)(2,1)}, u32[]{:S(2)}) copy-start(bf16[16,512]{1,0:T(8,128)(2,1)} %get-tuple-element.58) | copy-start | bytes 49156
  105.6 28.9 %all-to-all-start.3 = ((bf16[64,8,768]{2,1,0:T(8,128)(2,1)}), bf16[64,8,768]{2,1,0:T(8,128)(2,1)S(1)}, u32[]{:S(2)}, u32[]{:S(2)}) async-start(bf16[64,8,768]{2,1,0:T(8,128)(2,1)} %bitcast.12), calls=%async_computation.3 | async-start | bytes 1572864 | tf_op jit(solution)/shard_map/all_to_all | solution.py:401
